TPU v7x, 128 devices: a whole 4x4x4 slice. The times are simulated.
128 devices in a mesh: trow: 16 (over y, z), tcol: 8 (over x, core).
Axes of the slice: x: 4, y: 4, z: 4, core: 2. Of those that a mesh axis runs over, the one named last changes fastest.
Arguments:
- mask_level: float32 [16384, 16384], P('trow', 'tcol'), may hold values from -8 to 8
- target: bfloat16 [16384, 16384], P('trow', 'tcol'), may hold values from 0 to 1
- kernels: float32 [12, 2, 128, 128], replicated, may hold values from -2.2888184e-05 to 2.2888184e-05
- step_sizes: float32 [3], replicated, may hold values from 0.25 to 2
- density_class: int32 [32, 32], P('trow', 'tcol'), may hold values from 0 to 3, as said below
- work_list: int32 [128], replicated, may hold values from 0 to 1023, as said below
Outputs:
- mask_level_new: float32 [16384, 16384], P('trow', 'tcol')
Inputs may be any that keep to these rules, and one draw needn't show every extreme that they name: `density_class`: exactly 128 tiles are busy (class 1 to 3); the others are empty (class 0). The 2 x 4 tiles held by one device (tile rows 2 r, 2 r + 1 and tile columns 4 c .. 4 c + 3) hold at most 4 busy tiles, and some device's tiles hold exactly 4. `work_list`: entry d is the number a * 32 + b of the busy tile that device d computes, devices counted with trow slowest; its entries are distinct and are exactly the busy tiles.
All inputs are finite; a program needn't handle non-finite values.
Results may differ from a plain program's by a relative error of at most 0.005.
Values may be sent and summed in bfloat16 or wider, within the bound.
A program may use at most 128 MiB of HBM per device.

v0:
```python
import math

import jax
import jax.numpy as jnp
from jax import lax
from jax.sharding import PartitionSpec as P

APRON = 64
LEVELS = 3
MOST = 4


RESIST_SLOPE = 4.0
RESIST_LEVEL = 1.0


def with_halo(cells, sides, width):
    for axis, dim in sides:
        count = lax.axis_size(axis)
        ends = count - 1
        head = lax.slice_in_dim(cells, 0, width, axis=dim)
        tail = lax.slice_in_dim(cells, cells.shape[dim] - width, cells.shape[dim], axis=dim)
        cells = jnp.concatenate(
            [
                lax.ppermute(tail, axis, [(i, (i + 1) % count) for i in range(ends)]),
                cells,
                lax.ppermute(head, axis, [((i + 1) % count, i) for i in range(ends)]),
            ],
            axis=dim,
        )
    return cells


def spectral_tables(pad_side, tile_side, freq_count):
    freq_index = jnp.arange(freq_count, dtype=jnp.int32) - freq_count // 2
    positions = jnp.arange(pad_side, dtype=jnp.int32)
    turns = freq_index[:, None] * positions[None, :] % pad_side
    angles = turns.astype(jnp.float32) * (2.0 * math.pi / pad_side)
    cosines = jnp.cos(angles).astype(jnp.bfloat16)
    sines = jnp.sin(angles).astype(jnp.bfloat16)
    margin = (pad_side - tile_side) // 2
    return (
        cosines,
        sines,
        cosines[:, margin : margin + tile_side],
        sines[:, margin : margin + tile_side],
    )


def tile_gradient(extended, target_tile, kernels):
    pad_side = extended.shape[0]
    tile_side = target_tile.shape[0]
    freq_count = kernels.shape[-1]
    cosines, sines, core_cos, core_sin = spectral_tables(pad_side, tile_side, freq_count)
    full_rows = jnp.concatenate([cosines, sines], 0)
    row_spectra = jnp.dot(full_rows, extended, preferred_element_type=jnp.float32).astype(
        jnp.bfloat16
    )
    blocks = jnp.dot(row_spectra, full_rows.T, preferred_element_type=jnp.float32)
    spec_re = blocks[:freq_count, :freq_count] - blocks[freq_count:, freq_count:]
    spec_im = -(blocks[:freq_count, freq_count:] + blocks[freq_count:, :freq_count])
    inverse_right = jnp.concatenate([core_cos, core_sin], 1)
    inverse_rows = jnp.concatenate([core_cos, core_sin], 0)
    inverse_left = inverse_rows.T

    def half_inverse(part_re, part_im):
        stacked = jnp.concatenate([part_re, part_im], 0)
        product = jnp.dot(stacked, inverse_right, preferred_element_type=jnp.float32)
        out_re = product[:freq_count, :tile_side] - product[freq_count:, tile_side:]
        out_im = product[:freq_count, tile_side:] + product[freq_count:, :tile_side]
        return (out_re.astype(jnp.bfloat16), out_im.astype(jnp.bfloat16))

    def forward_kernel(carry, kernel):
        kern_re = kernel[0]
        kern_im = kernel[1]
        spec_z_re = (kern_re * spec_re - kern_im * spec_im).astype(jnp.bfloat16)
        spec_z_im = (kern_re * spec_im + kern_im * spec_re).astype(jnp.bfloat16)
        half_re, half_im = half_inverse(spec_z_re, spec_z_im)
        block = jnp.concatenate(
            [jnp.concatenate([half_re, half_im], 1), jnp.concatenate([-half_im, half_re], 1)], 0
        )
        field = jnp.dot(inverse_left, block, preferred_element_type=jnp.float32).astype(
            jnp.bfloat16
        )
        squares = field.astype(jnp.float32) ** 2
        return (carry + squares[:, :tile_side] + squares[:, tile_side:], field)

    intensity, fields = lax.scan(
        forward_kernel, jnp.zeros((tile_side, tile_side), jnp.float32), kernels
    )
    resist = jax.nn.sigmoid(RESIST_SLOPE * (intensity - RESIST_LEVEL))
    weight = (
        2.0 * (resist - target_tile.astype(jnp.float32)) * RESIST_SLOPE * resist * (1.0 - resist)
    )
    doubled = jnp.concatenate([2.0 * weight, 2.0 * weight], 1)

    def adjoint_kernel(carry, pair):
        kernel, field = pair
        kern_re = kernel[0]
        kern_im = kernel[1]
        pulled = (doubled * field.astype(jnp.float32)).astype(jnp.bfloat16)
        middle = jnp.dot(inverse_rows, pulled, preferred_element_type=jnp.float32)
        back_re = (middle[:freq_count, :tile_side] + middle[freq_count:, tile_side:]).astype(
            jnp.bfloat16
        )
        back_im = (middle[:freq_count, tile_side:] - middle[freq_count:, :tile_side]).astype(
            jnp.bfloat16
        )
        spectral = jnp.dot(
            jnp.concatenate([back_re, back_im], 0), inverse_left, preferred_element_type=jnp.float32
        )
        grad_re = spectral[:freq_count, :freq_count] + spectral[freq_count:, freq_count:]
        grad_im = spectral[freq_count:, :freq_count] - spectral[:freq_count, freq_count:]
        total_re = carry[0] + kern_re * grad_re + kern_im * grad_im
        total_im = carry[1] + kern_re * grad_im - kern_im * grad_re
        return ((total_re, total_im), None)

    empty = jnp.zeros((freq_count, freq_count), jnp.float32)
    totals, unused = lax.scan(adjoint_kernel, (empty, empty), (kernels, fields))
    last_re, last_im = half_inverse(totals[0].astype(jnp.bfloat16), totals[1].astype(jnp.bfloat16))
    return jnp.dot(
        inverse_left, jnp.concatenate([last_re, -last_im], 0), preferred_element_type=jnp.float32
    )


def deal_tiles(buffer):
    return lax.all_to_all(buffer, ("trow", "tcol"), split_axis=1, concat_axis=1, tiled=True)


def deal_grads(buffer):
    return lax.all_to_all(
        buffer.astype(jnp.bfloat16), ("trow", "tcol"), split_axis=1, concat_axis=1, tiled=True
    ).astype(buffer.dtype)


def body(mask_level, target, kernels, step_sizes, density_class, work_list):
    tile_side = target.shape[0] // 2
    col_slots = target.shape[1] // tile_side
    slot_count = 2 * col_slots
    pad_side = tile_side + 2 * APRON
    squashed = jax.nn.sigmoid(mask_level)
    trans = (2.0 * squashed - 1.0).astype(jnp.bfloat16)
    widened = with_halo(trans, (("trow", 0), ("tcol", 1)), APRON)
    slot_tiles = jnp.stack(
        [
            widened[
                r * tile_side : r * tile_side + pad_side, c * tile_side : c * tile_side + pad_side
            ]
            for r in range(2)
            for c in range(col_slots)
        ]
    )
    slot_targets = (
        target.reshape(2, tile_side, col_slots, tile_side)
        .transpose(0, 2, 1, 3)
        .reshape(slot_count, tile_side, tile_side)
    )
    local_class = density_class.reshape(slot_count)
    local_busy = (local_class > 0).astype(jnp.int32)
    local_rank = jnp.cumsum(local_busy) - local_busy
    slot_ids = jnp.arange(slot_count, dtype=jnp.int32)
    pack_match = local_busy[None, :] * (
        local_rank[None, :] == jnp.arange(MOST, dtype=jnp.int32)[:, None]
    ).astype(jnp.int32)
    packed_valid = jnp.sum(pack_match, 1)
    packed_slot = jnp.sum(pack_match * slot_ids[None, :], 1)
    valid_bf = packed_valid.astype(jnp.bfloat16)[:, None, None]
    packed_tiles = slot_tiles[packed_slot] * valid_bf
    packed_targets = slot_targets[packed_slot] * valid_bf
    col_devices = lax.axis_size("tcol")
    workers = lax.axis_size("trow") * col_devices
    tile_cols = col_slots * col_devices
    piece_tile = pad_side * pad_side // workers
    piece_goal = tile_side * tile_side // workers
    outgoing = jnp.concatenate(
        [
            packed_tiles.reshape(MOST, workers, piece_tile),
            packed_targets.reshape(MOST, workers, piece_goal),
        ],
        2,
    )
    collected = deal_tiles(outgoing)
    whole_class = lax.all_gather(local_class[None, :], ("trow", "tcol"), axis=0, tiled=True)
    device_busy = (whole_class > 0).astype(jnp.int32)
    device_rank = jnp.cumsum(device_busy, 1) - device_busy
    device_ids = jnp.arange(workers, dtype=jnp.int32)
    tile_number = (
        (device_ids[:, None] // col_devices * 2 + slot_ids[None, :] // col_slots) * tile_cols
        + device_ids[:, None] % col_devices * col_slots
        + slot_ids[None, :] % col_slots
    )
    matches = (tile_number[None, :, :] == work_list[:, None, None]).astype(jnp.int32)
    owner_of = jnp.sum(matches * device_ids[None, :, None], (1, 2))
    rank_of = jnp.sum(matches * device_rank[None, :, :], (1, 2))
    flat_rows = collected.reshape(MOST * workers, piece_tile + piece_goal)
    onward = flat_rows[rank_of * workers + owner_of][None]
    mine = deal_tiles(onward)[0]
    own_tile = mine[:, :piece_tile].reshape(pad_side, pad_side)
    own_target = mine[:, piece_tile:].reshape(tile_side, tile_side)
    own_grad = tile_gradient(own_tile, own_target, kernels)
    returned = deal_grads(own_grad.reshape(1, workers, piece_goal))[0]
    ranks_here = jnp.arange(MOST, dtype=jnp.int32)
    home_match = (
        (rank_of[None, None, :] == ranks_here[:, None, None])
        & (owner_of[None, None, :] == device_ids[None, :, None])
    ).astype(jnp.int32)
    helper_of = jnp.sum(home_match * device_ids[None, None, :], 2)
    filled = jnp.sum(home_match, 2).astype(jnp.float32)
    homeward = returned[helper_of] * filled[:, :, None]
    packed_grads = deal_grads(homeward).reshape(MOST, tile_side, tile_side)
    slot_grads = (
        packed_grads[jnp.minimum(local_rank, MOST - 1)]
        * local_busy.astype(jnp.float32)[:, None, None]
    )
    level_match = (
        local_class[:, None] == jnp.arange(1, LEVELS + 1, dtype=jnp.int32)[None, :]
    ).astype(jnp.float32)
    slot_steps = jnp.sum(level_match * step_sizes[None, :], 1)
    scaled = (
        (slot_steps[:, None, None] * slot_grads)
        .reshape(2, col_slots, tile_side, tile_side)
        .transpose(0, 2, 1, 3)
        .reshape(2 * tile_side, col_slots * tile_side)
    )
    return mask_level - scaled * (2.0 * squashed * (1.0 - squashed))


def solution(mesh):
    return jax.shard_map(
        body,
        mesh=mesh,
        in_specs=(P("trow", "tcol"), P("trow", "tcol"), P(), P(), P("trow", "tcol"), P()),
        out_specs=P("trow", "tcol"),
        check_vma=False,
    )
```

profile of v0, /device:TPU:1, one launch (start us, length us, event | category | flops | bytes accessed | tf_op | source)
XLA Modules:
  0.0 482.9 jit_solution(389080607338995761)
XLA Ops:
  0.0 4.6 add_convert_fusion.1
  6.6 4.4 collective-permute-start
  12.8 7.8 %reshape.403 = bf16[2,512,4,512]{3,2,1,0:T(4,128)(2,1)} reshape(bf16[1024,2048]{1,0:T(8,128)(2,1)} %param.11) | data formatting | bytes 8388608 | tf_op jit(solution)/shard_map/reshape | solution.py:154
  20.6 5.0 %copy.59 = bf16[2,4,512,512]{3,2,1,0:T(8,128)(2,1)} copy(bf16[2,4,512,512]{3,1,2,0:T(4,128)(2,1)} %bitcast.147) | data formatting | bytes 8388608 | tf_op jit(solution)/shard_map/transpose | solution.py:155
  25.7 4.2 gather_fusion.1
  34.3 4.1 collective-permute-start.2
  56.3 4.0 gather_fusion
  63.8 4.7 copy_multiply_fusion.1
  68.5 4.9 %pad_maximum_fusion = bf16[4,128,5248]{2,0,1:T(4,128)(2,1)} fusion(bf16[4,128,2048]{2,0,1:T(4,128)(2,1)S(1)} %copy-done.2, bf16[4,128,3200]{2,0,1:T(4,128)(2,1)S(1)} %copy_multiply_fusion.1), kind=kLoop, calls=%fused_computation.57 | loop fusion | flops 10747904 | bytes 10747904 | tf_op jit(solution)/shard_map/concatenate | solution.py:175
  73.5 10.9 %all-to-all-start = ((bf16[4,128,5248]{2,0,1:T(4,128)(2,1)}), bf16[4,128,5248]{2,0,1:T(4,128)(2,1)}, u32[]{:S(2)}, u32[]{:S(2)}) async-start(bf16[4,128,5248]{2,0,1:T(4,128)(2,1)} %pad_maximum_fusion), calls=%async_computation | async-start | bytes 10747904 | tf_op jit(solution)/shard_map/all_to_all | solution.py:127
  84.5 87.0 %all-gather = s32[128,1,8]{2,1,0:T(1,128)S(1)} all-gather(s32[1,1,8]{2,1,0:T(1,128)S(1)} %reshape.458), channel_id=1, replica_groups=mesh['trow'=16,'tcol'=8] {'trow','tcol'}, dimensions={0}, use_global_device_ids=true | all-gather | bytes 4128 | tf_op jit(solution)/shard_map/all_gather | solution.py:183
  171.9 4.9 %fusion.41 = (s32[128]{0:T(128)S(1)}, s32[128]{0:T(128)S(1)}) fusion(s32[128,8]{0,1:T(8,128)S(1)} %copy.62, s32[128,8]{0,1:T(8,128)S(1)} %add_add_fusion, s32[128]{0:T(128)S(1)} %copy-done.9), kind=kLoop, calls=%fused_computation.95 | loop fusion | flops 655104 | bytes 9728 | tf_op jit(solution)/shard_map/reduce_sum | solution.py:194
  176.8 5.5 %copy.61 = bf16[4,128,5248]{2,1,0:T(8,128)(2,1)} copy(bf16[4,128,5248]{2,0,1:T(4,128)(2,1)} %all-to-all-done) | data formatting | bytes 10747904 | tf_op jit(solution)/shard_map/all_to_all | solution.py:127
  182.2 7.0 %gather_fusion.2 = bf16[128,5248]{1,0:T(8,128)(2,1)} fusion(bf16[512,5248]{1,0:T(8,128)(2,1)} %bitcast.139, s32[1024]{0:T(1024)S(1)} %pad_clamp_fusion.2), kind=kCustom, calls=%fused_computation.2 | custom fusion | bytes 2687488 | tf_op jit(solution)/shard_map/gather | solution.py:196
  193.2 10.1 %reduce = bf16[128,5248]{1,0:T(8,128)(2,1)} reduce(bf16[128,1,5248]{2,1,0:T(2,128)(2,1)S(1)} %bitcast.148, bf16[]{:T(256)} %broadcast.475), dimensions={1}, to_apply=%bitcast.114.reduce_sub_computation | reduce | bytes 2686978
  203.2 4.2 reshape.466
  207.4 6.9 %all-to-all-start.1 = ((bf16[128,2,2624]{2,1,0:T(2,128)(2,1)}), bf16[128,2,2624]{2,1,0:T(2,128)(2,1)}, u32[]{:S(2)}, u32[]{:S(2)}) async-start(bf16[128,2,2624]{2,1,0:T(2,128)(2,1)} %reshape.466), calls=%async_computation.1 | async-start | bytes 2752512 | tf_op jit(solution)/shard_map/all_to_all | solution.py:127
  216.4 20.3 %all-to-all-done.1 = bf16[128,2,2624]{2,1,0:T(2,128)(2,1)} async-done(((bf16[128,2,2624]{2,1,0:T(2,128)(2,1)}), bf16[128,2,2624]{2,1,0:T(2,128)(2,1)}, u32[]{:S(2)}, u32[]{:S(2)}) %all-to-all-start.1) | async-done | bytes 1343520 | tf_op jit(solution)/shard_map/all_to_all | solution.py:127
  236.7 9.6 %reshape.467 = bf16[128,1,5248]{2,1,0:T(2,128)(2,1)} reshape(bf16[128,2,2624]{2,1,0:T(2,128)(2,1)} %all-to-all-done.1) | data formatting | bytes 2686976
  255.3 42.3 %while.26 = (s32[]{:T(128)}, f32[512,512]{0,1:T(8,128)S(1)}, bf16[12,512,1024]{1,2,0:T(8,128)(2,1)}, f32[12,2,128,128]{3,2,1,0:T(8,128)}, f32[128,128]{1,0:T(8,1...) while((s32[]{:T(128)}, f32[512,512]{0,1:T(8,128)S(1)}, ...), condition=%wide.region_8.9_spmd.clone, body=%wide.region_7.8_spmd.clone.sunk | while | flops 340590592 | bytes 13238423 | solution.py:88
  301.1 62.2 %while.27 = (s32[]{:T(128)}, f32[128,128]{1,0:T(8,128)S(1)}, f32[128,128]{1,0:T(8,128)S(1)}, f32[12,2,128,128]{3,2,1,0:T(8,128)}, bf16[12,512,1024]{1,2,0:T(8,12...) while((s32[]{:T(128)}, f32[128,128]{1,0:T(8,128)S(1)}, ...), condition=%wide.region_10.11_spmd.clone, body=%wide.region_9.10_spmd.clone.sunk | while | flops 338100224 | bytes 11403415 | solution.py:119
  369.3 4.6 all-to-all-start.2
  374.2 13.4 %all-to-all-done.2 = bf16[128,2,1024]{2,1,0:T(2,128)(2,1)S(1)} async-done(((bf16[128,2,1024]{2,1,0:T(2,128)(2,1)}), bf16[128,2,1024]{2,1,0:T(2,128)(2,1)S(1)}, u32[]{:S(2)}, u32[]{:S(2)}) %all-to-all-start.2) | async-done | bytes 524320 | tf_op jit(solution)/shard_map/all_to_all | solution.py:131
  392.0 6.5 %fusion.27 = bf16[4,128,2048]{2,0,1:T(4,128)(2,1)} fusion(f32[4,128,2048]{2,1,0:T(8,128)} %bitcast.146, f32[4,128]{0,1:T(8,128)S(1)} %copy.69), kind=kLoop, calls=%fused_computation.59 | loop fusion | flops 2097152 | bytes 6293504 | tf_op jit(solution)/shard_map/convert_element_type | solution.py:132
  398.6 4.5 all-to-all-start.3
  403.3 30.3 %all-to-all-done.3 = bf16[4,128,2048]{2,0,1:T(4,128)(2,1)S(1)} async-done(((bf16[4,128,2048]{2,0,1:T(4,128)(2,1)}), bf16[4,128,2048]{2,0,1:T(4,128)(2,1)S(1)}, u32[]{:S(2)}, u32[]{:S(2)}) %all-to-all-start.3) | async-done | bytes 2097184 | tf_op jit(solution)/shard_map/all_to_all | solution.py:131
  436.8 5.4 %reshape.416 = f32[4,512,512]{2,1,0:T(8,128)} reshape(f32[4,128,2048]{2,1,0:T(8,128)} %copy_convert_fusion) | data formatting | bytes 8388608 | tf_op jit(solution)/shard_map/reshape | solution.py:210
  442.2 6.7 %gather_fusion.4 = f32[8,512,512]{2,1,0:T(8,128)} fusion(f32[4,512,512]{2,1,0:T(8,128)} %reshape.416, s32[1024]{0:T(1024)S(1)} %pad_clamp_fusion), kind=kCustom, calls=%fused_computation.4 | custom fusion | bytes 16777248 | tf_op jit(solution)/shard_map/gather | solution.py:212
  448.9 8.8 %multiply_bitcast_fusion = f32[2,512,4,512]{3,1,2,0:T(8,128)} fusion(f32[2,4,512,512]{3,2,1,0:T(8,128)} %bitcast.143, f32[2,4]{1,0:T(2,128)S(1)} %get-tuple-element.259, f32[2,4]{1,0:T(2,128)S(1)} %mul.257), kind=kLoop, calls=%fused_computation.54 | loop fusion | flops 4194304 | bytes 16777280 | tf_op jit(solution)/shard_map/transpose | solution.py:222
  457.7 12.1 %copy.72 = f32[2,512,4,512]{3,2,1,0:T(4,128)} copy(f32[2,512,4,512]{3,1,2,0:T(8,128)} %multiply_bitcast_fusion) | data formatting | bytes 16777216 | tf_op jit(solution)/shard_map/transpose | solution.py:222
  469.8 7.7 %copy.75 = f32[128,8,4,512]{3,1,2,0:T(8,128)S(1)} copy(f32[128,8,4,512]{3,2,1,0:T(4,128)} %bitcast.144) | data formatting | bytes 16777216
  477.5 5.1 %multiply_subtract_fusion = f32[1024,2048]{1,0:T(8,128)} fusion(f32[1024,2048]{1,0:T(8,128)S(1)} %bitcast.141, f32[1024,2048]{1,0:T(8,128)S(1)} %bitcast.142), kind=kLoop, calls=%fused_computation.53 | loop fusion | flops 16777216 | bytes 25165824 | tf_op jit(solution)/shard_map/sub | solution.py:225
  (271 shorter events, 166.0 us)
Async XLA Ops:
  0.0 12.3 %copy-start.8 = (s32[2,4]{1,0:T(2,128)S(1)}, s32[2,4]{1,0:T(2,128)}, u32[]{:S(2)}) copy-start(s32[2,4]{1,0:T(2,128)} %param.14) | copy-start | bytes 100
  4.6 2.0 copy-start
  6.6 26.4 %collective-permute-start = (bf16[64,2048]{1,0:T(8,128)(2,1)S(1)}, bf16[64,2048]{1,0:T(8,128)(2,1)S(1)}, u32[]{:S(2)}, u32[]{:S(2)}) collective-permute-start(bf16[64,2048]{1,0:T(8,128)(2,1)S(1)} %get-tuple-element.255), channel_id=1, source_target_pairs={{0,8},{8,16},{16,24},{24,32},{32,40},{40,48},{48,56},{56,64},{64,7... | collective-permute-start | bytes 786440 | tf_op jit(solution)/shard_map/ppermute | solution.py:25
  11.0 22.0 %collective-permute-start.1 = (bf16[64,2048]{1,0:T(8,128)(2,1)S(1)}, bf16[64,2048]{1,0:T(8,128)(2,1)S(1)}, u32[]{:S(2)}, u32[]{:S(2)}) collective-permute-start(bf16[64,2048]{1,0:T(8,128)(2,1)S(1)} %get-tuple-element.256), channel_id=1, source_target_pairs={{8,0},{16,8},{24,16},{32,24},{40,32},{48,40},{56,48},{64,56},{72,6... | collective-permute-start | bytes 786440 | tf_op jit(solution)/shard_map/ppermute | solution.py:27
  33.0 10.8 %copy-start.1 = (bf16[1024,2048]{1,0:T(8,128)(2,1)S(1)}, bf16[1024,2048]{1,0:T(8,128)(2,1)}, u32[]{:S(2)}) copy-start(bf16[1024,2048]{1,0:T(8,128)(2,1)} %copy-done) | copy-start | bytes 12582916
  34.3 9.4 %collective-permute-start.2 = (bf16[1152,64]{1,0:T(8,128)(2,1)S(1)}, bf16[1152,64]{1,0:T(8,128)(2,1)S(1)}, u32[]{:S(2)}, u32[]{:S(2)}) collective-permute-start(bf16[1152,64]{1,0:T(8,128)(2,1)S(1)} %get-tuple-element.254), channel_id=1, source_target_pairs={{0,1},{1,2},{2,3},{3,4},{4,5},{5,6},{6,7},{8,9},{9,10},{10,11},{11... | collective-permute-start | bytes 442376 | tf_op jit(solution)/shard_map/ppermute | solution.py:25
  41.4 8.0 %collective-permute-start.3 = (bf16[1152,64]{1,0:T(8,128)(2,1)S(1)}, bf16[1152,64]{1,0:T(8,128)(2,1)S(1)}, u32[]{:S(2)}, u32[]{:S(2)}) collective-permute-start(bf16[1152,64]{1,0:T(8,128)(2,1)S(1)} %get-tuple-element.253), channel_id=1, source_target_pairs={{1,0},{2,1},{3,2},{4,3},{5,4},{6,5},{7,6},{9,8},{10,9},{11,10},{12... | collective-permute-start | bytes 442376 | tf_op jit(solution)/shard_map/ppermute | solution.py:27
  63.8 4.7 copy-start.2
  73.5 98.4 %copy-start.9 = (s32[128]{0:T(128)S(1)}, s32[128]{0:T(128)}, u32[]{:S(2)}) copy-start(s32[128]{0:T(128)} %param.15) | copy-start | bytes 1540
  73.5 103.3 %all-to-all-start = ((bf16[4,128,5248]{2,0,1:T(4,128)(2,1)}), bf16[4,128,5248]{2,0,1:T(4,128)(2,1)}, u32[]{:S(2)}, u32[]{:S(2)}) async-start(bf16[4,128,5248]{2,0,1:T(4,128)(2,1)} %pad_maximum_fusion), calls=%async_computation | async-start | bytes 10747904 | tf_op jit(solution)/shard_map/all_to_all | solution.py:127
  207.4 29.3 %all-to-all-start.1 = ((bf16[128,2,2624]{2,1,0:T(2,128)(2,1)}), bf16[128,2,2624]{2,1,0:T(2,128)(2,1)}, u32[]{:S(2)}, u32[]{:S(2)}) async-start(bf16[128,2,2624]{2,1,0:T(2,128)(2,1)} %reshape.466), calls=%async_computation.1 | async-start | bytes 2752512 | tf_op jit(solution)/shard_map/all_to_all | solution.py:127
  216.1 32.2 %copy-start.4 = (bf16[128,512]{1,0:T(8,128)(2,1)}, bf16[128,512]{1,0:T(8,128)(2,1)S(1)}, u32[]{:S(2)}) copy-start(bf16[128,512]{1,0:T(8,128)(2,1)S(1)} %slice.208) | copy-start | bytes 393220
  216.2 32.1 %copy-start.6 = (bf16[128,512]{1,0:T(8,128)(2,1)}, bf16[128,512]{1,0:T(8,128)(2,1)S(1)}, u32[]{:S(2)}) copy-start(bf16[128,512]{1,0:T(8,128)(2,1)S(1)} %slice.209) | copy-start | bytes 393220
  297.6 3.6 copy-start.3
  301.1 62.2 %copy-start.5 = (bf16[128,512]{1,0:T(8,128)(2,1)S(1)}, bf16[128,512]{1,0:T(8,128)(2,1)}, u32[]{:S(2)}) copy-start(bf16[128,512]{1,0:T(8,128)(2,1)} %copy-done.4) | copy-start | bytes 393220
  301.1 62.2 %copy-start.7 = (bf16[128,512]{1,0:T(8,128)(2,1)S(1)}, bf16[128,512]{1,0:T(8,128)(2,1)}, u32[]{:S(2)}) copy-start(bf16[128,512]{1,0:T(8,128)(2,1)} %copy-done.6) | copy-start | bytes 393220
  369.3 18.4 %all-to-all-start.2 = ((bf16[128,2,1024]{2,1,0:T(2,128)(2,1)}), bf16[128,2,1024]{2,1,0:T(2,128)(2,1)S(1)}, u32[]{:S(2)}, u32[]{:S(2)}) async-start(bf16[128,2,1024]{2,1,0:T(2,128)(2,1)} %reshape.468), calls=%async_computation.2 | async-start | bytes 1048576 | tf_op jit(solution)/shard_map/all_to_all | solution.py:131
  392.0 11.0 %copy-start.10 = (f32[3]{0:T(128)S(1)}, f32[3]{0:T(128)}, u32[]{:S(2)}) copy-start(f32[3]{0:T(128)} %param.13) | copy-start | bytes 40
  398.6 35.0 %all-to-all-start.3 = ((bf16[4,128,2048]{2,0,1:T(4,128)(2,1)}), bf16[4,128,2048]{2,0,1:T(4,128)(2,1)S(1)}, u32[]{:S(2)}, u32[]{:S(2)}) async-start(bf16[4,128,2048]{2,0,1:T(4,128)(2,1)} %fusion.27), calls=%async_computation.3 | async-start | bytes 4194304 | tf_op jit(solution)/shard_map/all_to_all | solution.py:131
  457.7 19.8 %slice-start = ((s8[8388608]{0:T(1024)(128)(4,1)}), s8[4194304]{0:T(1024)(128)(4,1)S(1)}, s32[]{:S(2)}) async-start(s8[8388608]{0:T(1024)(128)(4,1)} %bitcast.140), calls=%async_computation.4 | async-start | bytes 8388608
  469.8 7.7 %slice-start.1 = ((s8[8388608]{0:T(1024)(128)(4,1)}), s8[4194304]{0:T(1024)(128)(4,1)S(1)}, s32[]{:S(2)}) async-start(s8[8388608]{0:T(1024)(128)(4,1)} %bitcast.140), calls=%async_computation.5 | async-start | bytes 8388608
where the time goes:
time: 491 us; the launch traced here: 483 us
  local copies, waits for them, and re-layouts  139 us (28%)
  other arithmetic  111 us (23%)
  blocking collectives  87 us (18%)
  waiting for transfers between devices  65.7 us (13%)
  starting transfers between devices  39 us (8%)
  matrix products  39 us (8%)
    all_gather x1, blocking collectives, body(): lax.all_gather(local_class[None, :], ('trow', 'tcol'), axis=0, tiled=True)  87 us
    all_to_all x2, waiting for transfers between devices, deal_grads(): lax.all_to_all(buffer.astype(jnp.bfloat16), ('trow', 'tcol'), split_axis=...  43.7 us
    unnamed x34, local copies, waits for them, and re-layouts  27.6 us
    dot_general x12, matrix products, adjoint_kernel(): middle = jnp.dot(inverse_rows, pulled, preferred_element_type=jnp.float32)  24.6 us
    unnamed x13, other arithmetic  23.2 us
    dynamic_slice x24, local copies, waits for them, and re-layouts, tile_gradient(): totals, unused = lax.scan(adjoint_kernel, (empty, empty), (kernels, fields))  22 us
    all_to_all x2, waiting for transfers between devices, deal_tiles(): lax.all_to_all(buffer, ('trow', 'tcol'), split_axis=1, concat_axis=1, til...  20.3 us
    all_to_all x2, starting transfers between devices, deal_tiles(): lax.all_to_all(buffer, ('trow', 'tcol'), split_axis=1, concat_axis=1, til...  17.8 us
  transfers between devices with their start and end apart: 8, of which 4 were waited for; matrix products, arithmetic and copies ran while one was open for 7% of the time, Pallas kernels for 0%

commit v1 on v0

v1 whole, which is shorter than its diff:
```python
import functools

import jax
import jax.numpy as jnp
import ml_dtypes
import numpy as np
from jax import lax
from jax.experimental import pallas as pl
from jax.experimental.pallas import tpu as pltpu
from jax.sharding import PartitionSpec as P

TILE = 512
APRON = 64
PAD = TILE + 2 * APRON
FREQ = 128
KERNELS = 12
MOST = 4
SLOTS = 8
COLS = 4
GRID = 256
SIDE = 128
WIDE = TILE + 2 * SIDE
ROWS_HERE = 2 * TILE
COLS_HERE = COLS * TILE
BF = jnp.bfloat16
F32 = jnp.float32


def tables():
    freq = np.arange(FREQ, dtype=np.int64) - FREQ // 2

    def waves(count, period):
        turns = (freq[:, None] * np.arange(count)[None, :]) % period
        angles = turns * (2.0 * np.pi / period)
        return np.cos(angles), np.sin(angles)

    cos, sin = waves(PAD, PAD)
    spread = np.zeros((WIDE, 2 * FREQ))
    spread[SIDE - APRON : SIDE + TILE + APRON] = np.concatenate([cos, sin], 0).T
    rows = np.concatenate([cos, sin], 0)
    cg, sg = waves(GRID, GRID)
    coarse = np.block([[cg, sg], [-sg, cg]])
    core_cos, core_sin = cos[:, APRON : APRON + TILE], sin[:, APRON : APRON + TILE]
    fine = np.block([[core_cos, core_sin], [-core_sin, core_cos]])
    back = np.concatenate([core_cos, -core_sin], 0).T
    gap = np.arange(APRON, APRON + TILE)[:, None] - np.arange(GRID)[None, :] * (PAD / GRID)
    degree = np.arange(1, FREQ)
    lift = 1.0 + 2.0 * np.cos(gap[:, :, None] * degree * (2.0 * np.pi / PAD)).sum(2)
    lift = lift / GRID
    return [
        np.ascontiguousarray(t).astype(ml_dtypes.bfloat16)
        for t in (spread, rows, coarse, coarse.T, lift, lift.T, fine, back)
    ]


TABLE_SHAPES = (
    (WIDE, 2 * FREQ),
    (2 * FREQ, PAD),
    (2 * FREQ, 2 * GRID),
    (2 * GRID, 2 * FREQ),
    (TILE, GRID),
    (GRID, TILE),
    (2 * FREQ, 2 * TILE),
    (TILE, 2 * FREQ),
)


def dot(a, b):
    return jnp.dot(a, b, preferred_element_type=F32)


def step_kernel(
    cls_ref,
    steps_ref,
    mask_hbm,
    target_hbm,
    wide_hbm,
    kern_hbm,
    *rest,
):
    n_tab = len(TABLE_SHAPES)
    tab_hbm, rest = rest[:n_tab], rest[n_tab:]
    out_hbm = rest[0]
    (
        slot_ref,
        kern,
        ext,
        goal,
        mask,
        result,
        zbuf,
        wbuf,
        field,
        inten,
        tab_sem,
        kern_sem,
        ext_sem,
        goal_sem,
        mask_sem,
        out_sem,
        keep_sem,
        *tabs,
    ) = rest[1:]
    spread, rows, coarse, coarse_t, lift, lift_t, fine, back = tabs

    count = jnp.int32(0)
    for s in range(SLOTS):
        busy = cls_ref[s // COLS, s % COLS] > 0

        @pl.when(busy)
        def _(s=s, count=count):
            slot_ref[count] = s

        count = count + busy.astype(jnp.int32)

    def corner(s):
        r, c = s // COLS, s % COLS
        return pl.multiple_of(r * TILE, TILE), pl.multiple_of(c * TILE, TILE)

    def ext_copy(i):
        r, c = corner(slot_ref[i])
        return pltpu.make_async_copy(
            wide_hbm.at[pl.ds(r, PAD), pl.ds(c, WIDE)], ext.at[i], ext_sem.at[i]
        )

    def goal_copy(i):
        r, c = corner(slot_ref[i])
        return pltpu.make_async_copy(
            target_hbm.at[pl.ds(r, TILE), pl.ds(c, TILE)], goal.at[i], goal_sem.at[i]
        )

    def mask_copy(i):
        r, c = corner(slot_ref[i])
        return pltpu.make_async_copy(
            mask_hbm.at[pl.ds(r, TILE), pl.ds(c, TILE)], mask.at[i], mask_sem.at[i]
        )

    def out_copy(i):
        r, c = corner(slot_ref[i])
        return pltpu.make_async_copy(
            result.at[i], out_hbm.at[pl.ds(r, TILE), pl.ds(c, TILE)], out_sem.at[i]
        )

    def keep_copy(s):
        r, c = (s // COLS) * TILE, (s % COLS) * TILE
        return pltpu.make_async_copy(
            mask_hbm.at[pl.ds(r, TILE), pl.ds(c, TILE)],
            out_hbm.at[pl.ds(r, TILE), pl.ds(c, TILE)],
            keep_sem.at[s],
        )

    def tab_copy(t):
        return pltpu.make_async_copy(tab_hbm[t], tabs[t], tab_sem.at[t])

    kern_copy = pltpu.make_async_copy(kern_hbm, kern, kern_sem)

    tab_copy(0).start()

    @pl.when(count > 0)
    def _():
        ext_copy(0).start()

    tab_copy(1).start()
    kern_copy.start()
    for t in range(2, n_tab):
        tab_copy(t).start()

    @pl.when(count > 0)
    def _():
        goal_copy(0).start()
        mask_copy(0).start()

    def fetch(i, _):
        ext_copy(i).start()
        goal_copy(i).start()
        mask_copy(i).start()
        return 0

    lax.fori_loop(1, count, fetch, 0)
    for s in range(SLOTS):

        @pl.when(cls_ref[s // COLS, s % COLS] <= 0)
        def _(s=s):
            keep_copy(s).start()

    for t in range(n_tab):
        tab_copy(t).wait()
    kern_copy.wait()

    def tile(i, _):
        ext_copy(i).wait()
        first = dot(ext[i], spread[...]).astype(BF)
        blocks = dot(rows[...], first)
        spec_re = blocks[:FREQ, :FREQ] - blocks[FREQ:, FREQ:]
        spec_im = -(blocks[:FREQ, FREQ:] + blocks[FREQ:, :FREQ])

        for k in range(KERNELS):
            h_re, h_im = kern[k, 0], kern[k, 1]
            z_re = (h_re * spec_re - h_im * spec_im).astype(BF)
            z_im = (h_re * spec_im + h_im * spec_re).astype(BF)
            w = dot(jnp.concatenate([z_re, z_im], 1), coarse[...]).astype(BF)
            f = dot(coarse_t[...], jnp.concatenate([w[:, :GRID], w[:, GRID:]], 0))
            field[k] = f.astype(BF)
            square = f[:GRID] * f[:GRID] + f[GRID:] * f[GRID:]
            if k == 0:
                inten[...] = square - 1.0
            else:
                inten[...] += square

        goal_copy(i).wait()
        half = dot(lift[...], inten[...].astype(BF)).astype(BF)
        above = dot(half, lift_t[...])
        resist = 0.5 + 0.5 * jnp.tanh(2.0 * above)
        weight = (8.0 * (resist - goal[i].astype(F32))) * (resist * (1.0 - resist))
        drop = dot(lift_t[...], weight.astype(BF)).astype(BF)
        pull = (2.0 * dot(drop, lift[...])).astype(BF)

        tot_re = jnp.zeros((FREQ, FREQ), F32)
        tot_im = jnp.zeros((FREQ, FREQ), F32)
        for k in range(KERNELS):
            pulled = field[k] * jnp.concatenate([pull, pull], 0)
            y = dot(coarse[...], pulled).astype(BF)
            g = dot(jnp.concatenate([y[:FREQ], y[FREQ:]], 1), coarse_t[...])
            g_re, g_im = g[:, :FREQ], g[:, FREQ:]
            h_re, h_im = kern[k, 0], kern[k, 1]
            tot_re = tot_re + h_re * g_re + h_im * g_im
            tot_im = tot_im + h_re * g_im - h_im * g_re

        v = dot(jnp.concatenate([tot_re, tot_im], 1).astype(BF), fine[...]).astype(BF)
        grad = dot(back[...], jnp.concatenate([v[:, :TILE], v[:, TILE:]], 0))
        slot = slot_ref[i]
        level = cls_ref[slot // COLS, slot % COLS]
        size = 0.5 * steps_ref[level - 1]
        mask_copy(i).wait()
        here = mask[i]
        trans = jnp.tanh(0.5 * here)
        result[i] = here - (size * grad) * (1.0 - trans * trans)
        out_copy(i).start()
        return 0

    lax.fori_loop(0, count, tile, 0)

    def drain(i, _):
        out_copy(i).wait()
        return 0

    lax.fori_loop(0, count, drain, 0)
    for s in range(SLOTS):

        @pl.when(cls_ref[s // COLS, s % COLS] <= 0)
        def _(s=s):
            keep_copy(s).wait()


def take_step(cls, steps, mask, target, wide, kernels, tabs):
    any_spec = pl.BlockSpec(memory_space=pl.ANY)
    smem = pl.BlockSpec(memory_space=pltpu.SMEM)
    dma = pltpu.SemaphoreType.DMA
    return pl.pallas_call(
        step_kernel,
        out_shape=jax.ShapeDtypeStruct((ROWS_HERE, COLS_HERE), F32),
        in_specs=[smem, smem] + [any_spec] * (4 + len(TABLE_SHAPES)),
        out_specs=any_spec,
        scratch_shapes=[
            pltpu.SMEM((SLOTS,), jnp.int32),
            pltpu.VMEM((KERNELS, 2, FREQ, FREQ), F32),
            pltpu.VMEM((MOST, PAD, WIDE), BF),
            pltpu.VMEM((MOST, TILE, TILE), BF),
            pltpu.VMEM((MOST, TILE, TILE), F32),
            pltpu.VMEM((MOST, TILE, TILE), F32),
            pltpu.VMEM((KERNELS, FREQ, 2 * FREQ), BF),
            pltpu.VMEM((KERNELS, 2 * FREQ, GRID), BF),
            pltpu.VMEM((KERNELS, 2 * GRID, GRID), BF),
            pltpu.VMEM((GRID, GRID), F32),
            dma((len(TABLE_SHAPES),)),
            dma,
            dma((MOST,)),
            dma((MOST,)),
            dma((MOST,)),
            dma((MOST,)),
            dma((SLOTS,)),
        ]
        + [pltpu.VMEM(s, BF) for s in TABLE_SHAPES],
        compiler_params=pltpu.CompilerParams(vmem_limit_bytes=56 * 1024 * 1024),
        cost_estimate=pl.CostEstimate(
            flops=30_000_000_000, bytes_accessed=40_000_000, transcendentals=3_000_000
        ),
    )(cls, steps, mask, target, wide, kernels, *tabs)


CORNERS = ((-1, -1), (-1, 1), (1, -1), (1, 1))
SIDES = ((-1, 0), (1, 0), (0, -1), (0, 1)) + CORNERS
CHUNK = 128
CHUNKS = ROWS_HERE // CHUNK


def margin_kernel(
    n_rows,
    n_cols,
    mask_hbm,
    wide_hbm,
    rows_in,
    cols_in,
    rows_out,
    cols_out,
    corners_out,
    chunk_in,
    chunk_out,
    in_sem,
    chunk_sem,
    store_sem,
    send_sem,
    recv_sem,
):
    row, col = lax.axis_index("trow"), lax.axis_index("tcol")

    def near(dr, dc):
        return (lax.rem(row + dr + n_rows, n_rows), lax.rem(col + dc + n_cols, n_cols))

    barrier = pltpu.get_barrier_semaphore()
    for dr, dc in SIDES:
        pl.semaphore_signal(
            barrier, inc=1, device_id=near(dr, dc), device_id_type=pl.DeviceIdType.MESH
        )

    strips = []
    for side in range(2):
        start = side * (ROWS_HERE - APRON)
        strips.append(
            pltpu.make_async_copy(
                mask_hbm.at[pl.ds(start, APRON), :], rows_in.at[side], in_sem.at[side]
            )
        )
        start = side * (COLS_HERE - SIDE)
        strips.append(
            pltpu.make_async_copy(
                mask_hbm.at[:, pl.ds(start, SIDE)], cols_in.at[side], in_sem.at[2 + side]
            )
        )
    for copy in strips:
        copy.start()

    def load(n):
        return pltpu.make_async_copy(
            mask_hbm.at[pl.ds(n * CHUNK, CHUNK), :], chunk_in.at[n % 3], chunk_sem.at[n % 3]
        )

    def store(n):
        return pltpu.make_async_copy(
            chunk_out.at[n % 2],
            wide_hbm.at[pl.ds(APRON + n * CHUNK, CHUNK), pl.ds(SIDE, COLS_HERE)],
            store_sem.at[n % 2],
        )

    load(0).start()
    load(1).start()

    inside_r = [(row > 0).astype(F32), (row < n_rows - 1).astype(F32)]
    inside_c = [(col > 0).astype(F32), (col < n_cols - 1).astype(F32)]
    for copy in strips:
        copy.wait()
    for side in range(2):
        strip = jnp.tanh(0.5 * rows_in[side]) * inside_r[side]
        rows_out[side] = strip.astype(BF)
        for other in range(2):
            cut = strip[:, :SIDE] if other == 0 else strip[:, COLS_HERE - SIDE :]
            corners_out[2 * side + other] = (cut * inside_c[other]).astype(BF)
        cols_out[side] = (jnp.tanh(0.5 * cols_in[side]) * inside_c[side]).astype(BF)

    pl.semaphore_wait(barrier, len(SIDES))

    row_place = {-1: pl.ds(APRON + ROWS_HERE, APRON), 1: pl.ds(0, APRON), 0: pl.ds(APRON, ROWS_HERE)}
    col_place = {-1: pl.ds(SIDE + COLS_HERE, SIDE), 1: pl.ds(0, SIDE), 0: pl.ds(SIDE, COLS_HERE)}
    sources = [
        rows_out.at[0],
        rows_out.at[1],
        cols_out.at[0],
        cols_out.at[1],
    ] + [corners_out.at[n] for n in range(4)]
    sends = []
    for n, (dr, dc) in enumerate(SIDES):
        sends.append(
            pltpu.make_async_remote_copy(
                src_ref=sources[n],
                dst_ref=wide_hbm.at[row_place[dr], col_place[dc]],
                send_sem=send_sem.at[n],
                recv_sem=recv_sem.at[n],
                device_id=near(dr, dc),
                device_id_type=pl.DeviceIdType.MESH,
            )
        )
    for send in sends:
        send.start()

    for n in range(CHUNKS):
        if n + 2 < CHUNKS:
            load(n + 2).start()
        load(n).wait()
        if n >= 2:
            store(n - 2).wait()
        chunk_out[n % 2] = jnp.tanh(0.5 * chunk_in[n % 3]).astype(BF)
        store(n).start()
    store(CHUNKS - 2).wait()
    store(CHUNKS - 1).wait()
    for send in sends:
        send.wait()


def widen(mask, n_rows, n_cols):
    any_spec = pl.BlockSpec(memory_space=pl.ANY)
    dma = pltpu.SemaphoreType.DMA
    return pl.pallas_call(
        functools.partial(margin_kernel, n_rows, n_cols),
        out_shape=jax.ShapeDtypeStruct((ROWS_HERE + 2 * APRON, COLS_HERE + 2 * SIDE), BF),
        in_specs=[any_spec],
        out_specs=any_spec,
        scratch_shapes=[
            pltpu.VMEM((2, APRON, COLS_HERE), F32),
            pltpu.VMEM((2, ROWS_HERE, SIDE), F32),
            pltpu.VMEM((2, APRON, COLS_HERE), BF),
            pltpu.VMEM((2, ROWS_HERE, SIDE), BF),
            pltpu.VMEM((4, APRON, SIDE), BF),
            pltpu.VMEM((3, CHUNK, COLS_HERE), F32),
            pltpu.VMEM((2, CHUNK, COLS_HERE), BF),
            dma((4,)),
            dma((3,)),
            dma((2,)),
            dma((len(SIDES),)),
            dma((len(SIDES),)),
        ],
        compiler_params=pltpu.CompilerParams(
            collective_id=0, has_side_effects=True, vmem_limit_bytes=32 * 1024 * 1024
        ),
        cost_estimate=pl.CostEstimate(
            flops=10_000_000, bytes_accessed=14_000_000, transcendentals=2_000_000
        ),
    )(mask)


def body(mask_level, target, kernels, step_sizes, density_class, work_list):
    wide = widen(mask_level, lax.axis_size("trow"), lax.axis_size("tcol"))
    tabs = [jnp.asarray(t) for t in tables()]
    return take_step(density_class, step_sizes, mask_level, target, wide, kernels, tabs)


def solution(mesh):
    return jax.shard_map(
        body,
        mesh=mesh,
        in_specs=(P("trow", "tcol"), P("trow", "tcol"), P(), P(), P("trow", "tcol"), P()),
        out_specs=P("trow", "tcol"),
        check_vma=False,
    )
```

time: 491 us -> 278 us (0.57)
  the two profiles are of different devices: /device:TPU:1 before, /device:TPU:5 now
where the time goes in v1:
time: 278 us; the launch traced here: 277 us
  Pallas kernels  272 us (98%)
  local copies, waits for them, and re-layouts  5.69 us (2%)
    pallas_call x1, Pallas kernels, take_step(): pl.pallas_call(step_kernel, out_shape=jax.ShapeDtypeStruct((ROWS_HERE, CO...  256 us
    pallas_call x1, Pallas kernels, widen(): pl.pallas_call(functools.partial(margin_kernel, n_rows, n_cols), out_shap...  15.4 us
    unnamed x4, local copies, waits for them, and re-layouts  5.69 us

profile of v1, /device:TPU:5, one launch (start us, length us, event | category | flops | bytes accessed | tf_op | source)
XLA Modules:
  0.0 277.4 jit_solution(16828002520898916351)
XLA Ops:
  0.0 0.0 copy-start
  0.0 3.4 %copy-done = f32[1024,2048]{1,0:T(8,128)S(1)} copy-done((f32[1024,2048]{1,0:T(8,128)S(1)}, f32[1024,2048]{1,0:T(8,128)}, u32[]{:S(2)}) %copy-start) | copy-done | bytes 8388632
  3.4 15.4 %shard_map.127.wide_hbm = bf16[1152,2304]{1,0:T(8,128)(2,1)S(1)} custom-call(f32[1024,2048]{1,0:T(8,128)S(1)} %copy-done), custom_call_target="tpu_custom_call" | custom-call | flops 10000000 | bytes 14000000 | tf_op jit(solution)/shard_map/pallas_call | solution.py:412
  18.8 0.0 copy-start.1
  18.8 2.3 copy-done.1
  21.1 256.2 %shard_map.128 = f32[1024,2048]{1,0:T(8,128)} custom-call(s32[2,4]{1,0:T(2,128)} %cls_ref.1, f32[3]{0:T(128)} %steps_ref.1, f32[1024,2048]{1,0:T(8,128)} %mask_hbm.3, bf16[1024,2048]{1,0:T(8,128)(2,1)} %target_hbm.1, bf16[1152,2304]{1,0:T(8,128)(2,1)} %copy-done.1, f32[12,2,128,128]{3,2,1,0:T(8,128)} %kern_hbm.1, bf16[768,256]{1,0:T(8,128)(2,1)} %constant.16.clone.rest_0_, ...), custom_call_target="tpu_custom_call" | custom-call | flops 30000001024 | bytes 40000000 | tf_op jit(solution)/shard_map/pallas_call | solution.py:259
Async XLA Ops:
  0.0 3.4 %copy-start = (f32[1024,2048]{1,0:T(8,128)S(1)}, f32[1024,2048]{1,0:T(8,128)}, u32[]{:S(2)}) copy-start(f32[1024,2048]{1,0:T(8,128)} %mask_hbm.3) | copy-start | bytes 25165828
  18.8 2.3 copy-start.1

commit v2 on v1

--- a/solution.py
+++ b/solution.py
@@ -74,35 +74,26 @@
     steps_ref,
     mask_hbm,
     target_hbm,
-    wide_hbm,
-    kern_hbm,
-    *rest,
+    wide,
+    kern,
+    spread,
+    rows,
+    coarse,
+    coarse_t,
+    lift,
+    lift_t,
+    fine,
+    back,
+    out_hbm,
+    slot_ref,
+    goal,
+    mask,
+    field,
+    inten,
+    goal_sem,
+    mask_sem,
+    out_sem,
 ):
-    n_tab = len(TABLE_SHAPES)
-    tab_hbm, rest = rest[:n_tab], rest[n_tab:]
-    out_hbm = rest[0]
-    (
-        slot_ref,
-        kern,
-        ext,
-        goal,
-        mask,
-        result,
-        zbuf,
-        wbuf,
-        field,
-        inten,
-        tab_sem,
-        kern_sem,
-        ext_sem,
-        goal_sem,
-        mask_sem,
-        out_sem,
-        keep_sem,
-        *tabs,
-    ) = rest[1:]
-    spread, rows, coarse, coarse_t, lift, lift_t, fine, back = tabs
-
     count = jnp.int32(0)
     for s in range(SLOTS):
         busy = cls_ref[s // COLS, s % COLS] > 0
@@ -117,79 +108,42 @@
         r, c = s // COLS, s % COLS
         return pl.multiple_of(r * TILE, TILE), pl.multiple_of(c * TILE, TILE)
 
-    def ext_copy(i):
-        r, c = corner(slot_ref[i])
-        return pltpu.make_async_copy(
-            wide_hbm.at[pl.ds(r, PAD), pl.ds(c, WIDE)], ext.at[i], ext_sem.at[i]
-        )
-
     def goal_copy(i):
         r, c = corner(slot_ref[i])
         return pltpu.make_async_copy(
             target_hbm.at[pl.ds(r, TILE), pl.ds(c, TILE)], goal.at[i], goal_sem.at[i]
         )
 
-    def mask_copy(i):
-        r, c = corner(slot_ref[i])
-        return pltpu.make_async_copy(
-            mask_hbm.at[pl.ds(r, TILE), pl.ds(c, TILE)], mask.at[i], mask_sem.at[i]
-        )
-
-    def out_copy(i):
-        r, c = corner(slot_ref[i])
-        return pltpu.make_async_copy(
-            result.at[i], out_hbm.at[pl.ds(r, TILE), pl.ds(c, TILE)], out_sem.at[i]
-        )
-
-    def keep_copy(s):
+    def mask_copy(s):
         r, c = (s // COLS) * TILE, (s % COLS) * TILE
         return pltpu.make_async_copy(
-            mask_hbm.at[pl.ds(r, TILE), pl.ds(c, TILE)],
-            out_hbm.at[pl.ds(r, TILE), pl.ds(c, TILE)],
-            keep_sem.at[s],
-        )
-
-    def tab_copy(t):
-        return pltpu.make_async_copy(tab_hbm[t], tabs[t], tab_sem.at[t])
-
-    kern_copy = pltpu.make_async_copy(kern_hbm, kern, kern_sem)
-
-    tab_copy(0).start()
-
-    @pl.when(count > 0)
-    def _():
-        ext_copy(0).start()
-
-    tab_copy(1).start()
-    kern_copy.start()
-    for t in range(2, n_tab):
-        tab_copy(t).start()
-
-    @pl.when(count > 0)
-    def _():
-        goal_copy(0).start()
-        mask_copy(0).start()
+            mask_hbm.at[pl.ds(r, TILE), pl.ds(c, TILE)], mask.at[s], mask_sem.at[s]
+        )
+
+    def out_copy(s):
+        r, c = corner(s)
+        return pltpu.make_async_copy(
+            mask.at[s], out_hbm.at[pl.ds(r, TILE), pl.ds(c, TILE)], out_sem.at[s]
+        )
 
     def fetch(i, _):
-        ext_copy(i).start()
         goal_copy(i).start()
-        mask_copy(i).start()
         return 0
 
-    lax.fori_loop(1, count, fetch, 0)
+    lax.fori_loop(0, count, fetch, 0)
     for s in range(SLOTS):
+        mask_copy(s).start()
+    for s in range(SLOTS):
+        mask_copy(s).wait()
 
         @pl.when(cls_ref[s // COLS, s % COLS] <= 0)
         def _(s=s):
-            keep_copy(s).start()
-
-    for t in range(n_tab):
-        tab_copy(t).wait()
-    kern_copy.wait()
+            out_copy(s).start()
 
     def tile(i, _):
-        ext_copy(i).wait()
-        first = dot(ext[i], spread[...]).astype(BF)
+        slot = slot_ref[i]
+        r, c = corner(slot)
+        first = dot(wide[pl.ds(r, PAD), pl.ds(c, WIDE)], spread[...]).astype(BF)
         blocks = dot(rows[...], first)
         spec_re = blocks[:FREQ, :FREQ] - blocks[FREQ:, FREQ:]
         spec_im = -(blocks[:FREQ, FREQ:] + blocks[FREQ:, :FREQ])
@@ -228,64 +182,54 @@
 
         v = dot(jnp.concatenate([tot_re, tot_im], 1).astype(BF), fine[...]).astype(BF)
         grad = dot(back[...], jnp.concatenate([v[:, :TILE], v[:, TILE:]], 0))
-        slot = slot_ref[i]
         level = cls_ref[slot // COLS, slot % COLS]
         size = 0.5 * steps_ref[level - 1]
-        mask_copy(i).wait()
-        here = mask[i]
+        here = mask[slot]
         trans = jnp.tanh(0.5 * here)
-        result[i] = here - (size * grad) * (1.0 - trans * trans)
-        out_copy(i).start()
+        mask[slot] = here - (size * grad) * (1.0 - trans * trans)
+        out_copy(slot).start()
         return 0
 
     lax.fori_loop(0, count, tile, 0)
 
-    def drain(i, _):
-        out_copy(i).wait()
-        return 0
-
-    lax.fori_loop(0, count, drain, 0)
     for s in range(SLOTS):
-
-        @pl.when(cls_ref[s // COLS, s % COLS] <= 0)
-        def _(s=s):
-            keep_copy(s).wait()
+        out_copy(s).wait()
 
 
 def take_step(cls, steps, mask, target, wide, kernels, tabs):
-    any_spec = pl.BlockSpec(memory_space=pl.ANY)
+    hbm = pl.BlockSpec(memory_space=pltpu.HBM)
+    vmem = pl.BlockSpec(memory_space=pltpu.VMEM)
     smem = pl.BlockSpec(memory_space=pltpu.SMEM)
     dma = pltpu.SemaphoreType.DMA
+    here = pltpu.with_memory_space_constraint
     return pl.pallas_call(
         step_kernel,
         out_shape=jax.ShapeDtypeStruct((ROWS_HERE, COLS_HERE), F32),
-        in_specs=[smem, smem] + [any_spec] * (4 + len(TABLE_SHAPES)),
-        out_specs=any_spec,
+        in_specs=[smem, smem, hbm, hbm, vmem, vmem] + [vmem] * len(TABLE_SHAPES),
+        out_specs=hbm,
         scratch_shapes=[
             pltpu.SMEM((SLOTS,), jnp.int32),
-            pltpu.VMEM((KERNELS, 2, FREQ, FREQ), F32),
-            pltpu.VMEM((MOST, PAD, WIDE), BF),
             pltpu.VMEM((MOST, TILE, TILE), BF),
-            pltpu.VMEM((MOST, TILE, TILE), F32),
-            pltpu.VMEM((MOST, TILE, TILE), F32),
-            pltpu.VMEM((KERNELS, FREQ, 2 * FREQ), BF),
-            pltpu.VMEM((KERNELS, 2 * FREQ, GRID), BF),
+            pltpu.VMEM((SLOTS, TILE, TILE), F32),
             pltpu.VMEM((KERNELS, 2 * GRID, GRID), BF),
             pltpu.VMEM((GRID, GRID), F32),
-            dma((len(TABLE_SHAPES),)),
-            dma,
-            dma((MOST,)),
-            dma((MOST,)),
-            dma((MOST,)),
             dma((MOST,)),
             dma((SLOTS,)),
-        ]
-        + [pltpu.VMEM(s, BF) for s in TABLE_SHAPES],
-        compiler_params=pltpu.CompilerParams(vmem_limit_bytes=56 * 1024 * 1024),
+            dma((SLOTS,)),
+        ],
+        compiler_params=pltpu.CompilerParams(vmem_limit_bytes=32 * 1024 * 1024),
         cost_estimate=pl.CostEstimate(
             flops=30_000_000_000, bytes_accessed=40_000_000, transcendentals=3_000_000
         ),
-    )(cls, steps, mask, target, wide, kernels, *tabs)
+    )(
+        cls,
+        steps,
+        here(mask, pltpu.HBM),
+        here(target, pltpu.HBM),
+        here(wide, pltpu.VMEM),
+        here(kernels, pltpu.VMEM),
+        *[here(t, pltpu.VMEM) for t in tabs],
+    )
 
 
 CORNERS = ((-1, -1), (-1, 1), (1, -1), (1, 1))
@@ -298,7 +242,7 @@
     n_rows,
     n_cols,
     mask_hbm,
-    wide_hbm,
+    wide,
     rows_in,
     cols_in,
     rows_out,
@@ -348,7 +292,7 @@
     def store(n):
         return pltpu.make_async_copy(
             chunk_out.at[n % 2],
-            wide_hbm.at[pl.ds(APRON + n * CHUNK, CHUNK), pl.ds(SIDE, COLS_HERE)],
+            wide.at[pl.ds(APRON + n * CHUNK, CHUNK), pl.ds(SIDE, COLS_HERE)],
             store_sem.at[n % 2],
         )
 
@@ -382,7 +326,7 @@
         sends.append(
             pltpu.make_async_remote_copy(
                 src_ref=sources[n],
-                dst_ref=wide_hbm.at[row_place[dr], col_place[dc]],
+                dst_ref=wide.at[row_place[dr], col_place[dc]],
                 send_sem=send_sem.at[n],
                 recv_sem=recv_sem.at[n],
                 device_id=near(dr, dc),
@@ -407,13 +351,12 @@
 
 
 def widen(mask, n_rows, n_cols):
-    any_spec = pl.BlockSpec(memory_space=pl.ANY)
     dma = pltpu.SemaphoreType.DMA
     return pl.pallas_call(
         functools.partial(margin_kernel, n_rows, n_cols),
-        out_shape=jax.ShapeDtypeStruct((ROWS_HERE + 2 * APRON, COLS_HERE + 2 * SIDE), BF),
-        in_specs=[any_spec],
-        out_specs=any_spec,
+        out_shape=pltpu.VMEM((ROWS_HERE + 2 * APRON, COLS_HERE + 2 * SIDE), BF),
+        in_specs=[pl.BlockSpec(memory_space=pltpu.HBM)],
+        out_specs=pl.BlockSpec(memory_space=pltpu.VMEM),
         scratch_shapes=[
             pltpu.VMEM((2, APRON, COLS_HERE), F32),
             pltpu.VMEM((2, ROWS_HERE, SIDE), F32),
@@ -434,7 +377,7 @@
         cost_estimate=pl.CostEstimate(
             flops=10_000_000, bytes_accessed=14_000_000, transcendentals=2_000_000
         ),
-    )(mask)
+    )(pltpu.with_memory_space_constraint(mask, pltpu.HBM))
 
 
 def body(mask_level, target, kernels, step_sizes, density_class, work_list):

time: 278 us -> 53.8 us (0.19)
  the two profiles are of different devices: /device:TPU:5 before, /device:TPU:33 now
where the time goes in v2:
time: 53.8 us; the launch traced here: 53.6 us
  Pallas kernels  53.4 us (99%)
    pallas_call x1, Pallas kernels, take_step(): pl.pallas_call(step_kernel, out_shape=jax.ShapeDtypeStruct((ROWS_HERE, CO...  38.2 us
    pallas_call x1, Pallas kernels, widen(): pl.pallas_call(functools.partial(margin_kernel, n_rows, n_cols), out_shap...  15.3 us

profile of v2, /device:TPU:33, one launch (start us, length us, event | category | flops | bytes accessed | tf_op | source)
XLA Modules:
  0.0 53.6 jit_solution(9218223015574334622)
XLA Ops:
  0.0 0.0 copy-start.3
  0.0 0.0 copy-start.4
  0.0 0.0 copy-start.5
  0.0 0.0 copy-start.6
  0.0 0.0 copy-start.7
  0.0 0.0 copy-start.8
  0.0 0.0 copy-start.9
  0.1 0.0 copy-start.10
  0.1 0.0 copy-start.1
  0.1 0.0 copy-start.2
  0.1 0.0 copy-start
  0.1 15.3 %shard_map.127.wide = bf16[1152,2304]{1,0:T(8,128)(2,1)S(1)} custom-call(f32[1024,2048]{1,0:T(8,128)} %mask_hbm.3), custom_call_target="tpu_custom_call" | custom-call | flops 10000000 | bytes 14000000 | tf_op jit(solution)/shard_map/pallas_call | solution.py:355
  15.4 0.0 copy-done.3
  15.4 0.0 copy-done.4
  15.4 0.0 copy-done.5
  15.4 0.0 copy-done.6
  15.4 0.0 copy-done.7
  15.4 0.0 copy-done.8
  15.4 0.0 copy-done.9
  15.4 0.0 copy-done.10
  15.5 0.0 copy-done.1
  15.5 0.0 copy-done.2
  15.5 0.0 copy-done
  15.5 38.2 %shard_map.128 = f32[1024,2048]{1,0:T(8,128)} custom-call(s32[2,4]{1,0:T(2,128)S(1)} %copy-done.1, f32[3]{0:T(128)S(1)} %copy-done.2, f32[1024,2048]{1,0:T(8,128)} %mask_hbm.3, bf16[1024,2048]{1,0:T(8,128)(2,1)} %target_hbm.1, bf16[1152,2304]{1,0:T(8,128)(2,1)S(1)} %shard_map.127.wide, f32[12,2,128,128]{3,2,1,0:T(8,128)S(1)} %copy-done, ...), custom_call_target="tpu_custom_call" | custom-call | flops 30000001024 | bytes 40000000 | tf_op jit(solution)/shard_map/pallas_call | solution.py:205
Async XLA Ops:
  0.0 15.4 %copy-start.3 = (bf16[256,1024]{1,0:T(8,128)(2,1)S(1)}, bf16[256,1024]{1,0:T(8,128)(2,1)}, u32[]{:S(2)}) copy-start(bf16[256,1024]{1,0:T(8,128)(2,1)} %constant.22.clone.fine) | copy-start | bytes 1572868
  0.0 15.4 %copy-start.4 = (bf16[768,256]{1,0:T(8,128)(2,1)S(1)}, bf16[768,256]{1,0:T(8,128)(2,1)}, u32[]{:S(2)}) copy-start(bf16[768,256]{1,0:T(8,128)(2,1)} %constant.16.clone.spread) | copy-start | bytes 1179652
  0.0 15.4 %copy-start.5 = (bf16[256,640]{1,0:T(8,128)(2,1)S(1)}, bf16[256,640]{1,0:T(8,128)(2,1)}, u32[]{:S(2)}) copy-start(bf16[256,640]{1,0:T(8,128)(2,1)} %constant.17.clone.rows) | copy-start | bytes 983044
  0.0 15.4 %copy-start.6 = (bf16[512,256]{1,0:T(8,128)(2,1)S(1)}, bf16[512,256]{1,0:T(8,128)(2,1)}, u32[]{:S(2)}) copy-start(bf16[512,256]{1,0:T(8,128)(2,1)} %constant.23.clone.back) | copy-start | bytes 786436
  0.0 15.4 %copy-start.7 = (bf16[256,512]{1,0:T(8,128)(2,1)S(1)}, bf16[256,512]{1,0:T(8,128)(2,1)}, u32[]{:S(2)}) copy-start(bf16[256,512]{1,0:T(8,128)(2,1)} %constant.21.clone.lift_t) | copy-start | bytes 786436
  0.0 15.4 %copy-start.8 = (bf16[512,256]{1,0:T(8,128)(2,1)S(1)}, bf16[512,256]{1,0:T(8,128)(2,1)}, u32[]{:S(2)}) copy-start(bf16[512,256]{1,0:T(8,128)(2,1)} %constant.20.clone.lift) | copy-start | bytes 786436
  0.0 15.4 %copy-start.9 = (bf16[512,256]{1,0:T(8,128)(2,1)S(1)}, bf16[512,256]{1,0:T(8,128)(2,1)}, u32[]{:S(2)}) copy-start(bf16[512,256]{1,0:T(8,128)(2,1)} %constant.19.clone.coarse_t) | copy-start | bytes 786436
  0.1 15.4 %copy-start.10 = (bf16[256,512]{1,0:T(8,128)(2,1)S(1)}, bf16[256,512]{1,0:T(8,128)(2,1)}, u32[]{:S(2)}) copy-start(bf16[256,512]{1,0:T(8,128)(2,1)} %constant.18.clone.coarse) | copy-start | bytes 786436
  0.1 15.4 %copy-start.1 = (s32[2,4]{1,0:T(2,128)S(1)}, s32[2,4]{1,0:T(2,128)}, u32[]{:S(2)}) copy-start(s32[2,4]{1,0:T(2,128)} %cls_ref.1) | copy-start | bytes 100
  0.1 15.4 %copy-start.2 = (f32[3]{0:T(128)S(1)}, f32[3]{0:T(128)}, u32[]{:S(2)}) copy-start(f32[3]{0:T(128)} %steps_ref.1) | copy-start | bytes 40
  0.1 15.4 %copy-start = (f32[12,2,128,128]{3,2,1,0:T(8,128)S(1)}, f32[12,2,128,128]{3,2,1,0:T(8,128)}, u32[]{:S(2)}) copy-start(f32[12,2,128,128]{3,2,1,0:T(8,128)} %kern.1) | copy-start | bytes 4718596

commit v3 on v2

--- a/solution.py
+++ b/solution.py
@@ -16,6 +16,8 @@
 KERNELS = 12
 MOST = 4
 SLOTS = 8
+GROUP = 12
+LANES = 2
 COLS = 4
 GRID = 256
 SIDE = 128
@@ -88,11 +90,13 @@
     slot_ref,
     goal,
     mask,
+    result,
     field,
     inten,
     goal_sem,
     mask_sem,
     out_sem,
+    keep_sem,
 ):
     count = jnp.int32(0)
     for s in range(SLOTS):
@@ -120,10 +124,16 @@
             mask_hbm.at[pl.ds(r, TILE), pl.ds(c, TILE)], mask.at[s], mask_sem.at[s]
         )
 
-    def out_copy(s):
-        r, c = corner(s)
-        return pltpu.make_async_copy(
-            mask.at[s], out_hbm.at[pl.ds(r, TILE), pl.ds(c, TILE)], out_sem.at[s]
+    def keep_copy(s):
+        r, c = (s // COLS) * TILE, (s % COLS) * TILE
+        return pltpu.make_async_copy(
+            mask.at[s], out_hbm.at[pl.ds(r, TILE), pl.ds(c, TILE)], keep_sem.at[s]
+        )
+
+    def out_copy(i):
+        r, c = corner(slot_ref[i])
+        return pltpu.make_async_copy(
+            result.at[i], out_hbm.at[pl.ds(r, TILE), pl.ds(c, TILE)], out_sem.at[i]
         )
 
     def fetch(i, _):
@@ -133,67 +143,134 @@
     lax.fori_loop(0, count, fetch, 0)
     for s in range(SLOTS):
         mask_copy(s).start()
+
+    def keep():
+        for s in range(SLOTS):
+            mask_copy(s).wait()
+
+            @pl.when(cls_ref[s // COLS, s % COLS] <= 0)
+            def _(s=s):
+                keep_copy(s).start()
+
+    @pl.when(count == 0)
+    def _():
+        keep()
+
+    def spectrum(t):
+        first = dot(wide[pl.ds(t.r, PAD), pl.ds(t.c, WIDE)], spread[...]).astype(BF)
+        blocks = dot(rows[...], first)
+        re = blocks[:FREQ, :FREQ] - blocks[FREQ:, FREQ:]
+        im = -(blocks[:FREQ, FREQ:] + blocks[FREQ:, :FREQ])
+        t.spec_re = jnp.concatenate([re, re], 1)
+        t.spec_im = jnp.concatenate([im, im], 1)
+
+    def forward(t, k):
+        parts = []
+        for p in range(k, k + GROUP, 2):
+            h_re = jnp.concatenate([kern[p, 0], kern[p + 1, 0]], 1)
+            h_im = jnp.concatenate([kern[p, 1], kern[p + 1, 1]], 1)
+            z_re = (h_re * t.spec_re - h_im * t.spec_im).astype(BF)
+            z_im = (h_re * t.spec_im + h_im * t.spec_re).astype(BF)
+            w = dot(coarse_t[...], jnp.concatenate([z_re, z_im], 0)).astype(BF)
+            for n in range(2):
+                cut = w[:, n * FREQ : (n + 1) * FREQ]
+                parts.append(jnp.concatenate([cut[:GRID], cut[GRID:]], 1))
+        f = dot(jnp.concatenate(parts, 0), coarse[...])
+        total = None
+        for n in range(GROUP):
+            one = f[n * GRID : (n + 1) * GRID]
+            field[t.lane, k + n] = one.astype(BF)
+            square = one[:, :GRID] * one[:, :GRID] + one[:, GRID:] * one[:, GRID:]
+            total = square if total is None else total + square
+        if k == 0:
+            inten[t.lane] = total - 1.0
+        else:
+            inten[t.lane] += total
+
+    def resist(t):
+        half = dot(lift[...], (2.0 * inten[t.lane]).astype(BF)).astype(BF)
+        bend = jnp.tanh(dot(half, lift_t[...]))
+        weight = (1.0 + bend - 2.0 * goal[t.i].astype(F32)) * (1.0 - bend * bend)
+        drop = dot(lift_t[...], weight.astype(BF)).astype(BF)
+        pull = (2.0 * dot(drop, lift[...])).astype(BF)
+        t.pull = jnp.concatenate([pull, pull], 1)
+        t.tot_re = jnp.zeros((FREQ, 2 * FREQ), F32)
+        t.tot_im = jnp.zeros((FREQ, 2 * FREQ), F32)
+
+    def adjoint(t, k):
+        pulled = jnp.concatenate([field[t.lane, k + n] * t.pull for n in range(GROUP)], 0)
+        x = dot(pulled, coarse_t[...]).astype(BF)
+        for p in range(0, GROUP, 2):
+            a = x[p * GRID : (p + 1) * GRID]
+            b = x[(p + 1) * GRID : (p + 2) * GRID]
+            pair = jnp.concatenate(
+                [
+                    jnp.concatenate([a[:, :FREQ], b[:, :FREQ]], 1),
+                    jnp.concatenate([a[:, FREQ:], b[:, FREQ:]], 1),
+                ],
+                0,
+            )
+            g = dot(coarse[...], pair)
+            g_re, g_im = g[:FREQ], g[FREQ:]
+            h_re = jnp.concatenate([kern[k + p, 0], kern[k + p + 1, 0]], 1)
+            h_im = jnp.concatenate([kern[k + p, 1], kern[k + p + 1, 1]], 1)
+            t.tot_re = t.tot_re + h_re * g_re + h_im * g_im
+            t.tot_im = t.tot_im + h_re * g_im - h_im * g_re
+
+    def finish(t):
+        level = cls_ref[t.slot // COLS, t.slot % COLS]
+        size = 0.5 * steps_ref[level - 1]
+        tot_re = size * (t.tot_re[:, :FREQ] + t.tot_re[:, FREQ:])
+        tot_im = size * (t.tot_im[:, :FREQ] + t.tot_im[:, FREQ:])
+        v = dot(jnp.concatenate([tot_re, tot_im], 1).astype(BF), fine[...]).astype(BF)
+        grad = dot(back[...], jnp.concatenate([v[:, :TILE], v[:, TILE:]], 0))
+        here = mask[t.slot]
+        trans = jnp.tanh(0.5 * here)
+        result[t.i] = here - grad * (1.0 - trans * trans)
+
+    class Tile:
+        def __init__(self, i, lane):
+            self.i, self.lane = i, lane
+            self.slot = slot_ref[i]
+            self.r, self.c = corner(self.slot)
+
+    def batch(b, _):
+        start = b * LANES
+        tiles = [Tile(jnp.minimum(start + n, count - 1), n) for n in range(LANES)]
+        for t in tiles:
+            spectrum(t)
+        for k in range(0, KERNELS, GROUP):
+            for t in tiles:
+                forward(t, k)
+
+        @pl.when(b == 0)
+        def _():
+            keep()
+            lax.fori_loop(0, count, lambda i, _: (goal_copy(i).wait(), 0)[1], 0)
+
+        for t in tiles:
+            resist(t)
+        for k in range(0, KERNELS, GROUP):
+            for t in tiles:
+                adjoint(t, k)
+        for t in tiles:
+            finish(t)
+        for n in range(LANES):
+
+            @pl.when(start + n < count)
+            def _(n=n):
+                out_copy(start + n).start()
+
+        return 0
+
+    lax.fori_loop(0, (count + LANES - 1) // LANES, batch, 0)
+
+    lax.fori_loop(0, count, lambda i, _: (out_copy(i).wait(), 0)[1], 0)
     for s in range(SLOTS):
-        mask_copy(s).wait()
 
         @pl.when(cls_ref[s // COLS, s % COLS] <= 0)
         def _(s=s):
-            out_copy(s).start()
-
-    def tile(i, _):
-        slot = slot_ref[i]
-        r, c = corner(slot)
-        first = dot(wide[pl.ds(r, PAD), pl.ds(c, WIDE)], spread[...]).astype(BF)
-        blocks = dot(rows[...], first)
-        spec_re = blocks[:FREQ, :FREQ] - blocks[FREQ:, FREQ:]
-        spec_im = -(blocks[:FREQ, FREQ:] + blocks[FREQ:, :FREQ])
-
-        for k in range(KERNELS):
-            h_re, h_im = kern[k, 0], kern[k, 1]
-            z_re = (h_re * spec_re - h_im * spec_im).astype(BF)
-            z_im = (h_re * spec_im + h_im * spec_re).astype(BF)
-            w = dot(jnp.concatenate([z_re, z_im], 1), coarse[...]).astype(BF)
-            f = dot(coarse_t[...], jnp.concatenate([w[:, :GRID], w[:, GRID:]], 0))
-            field[k] = f.astype(BF)
-            square = f[:GRID] * f[:GRID] + f[GRID:] * f[GRID:]
-            if k == 0:
-                inten[...] = square - 1.0
-            else:
-                inten[...] += square
-
-        goal_copy(i).wait()
-        half = dot(lift[...], inten[...].astype(BF)).astype(BF)
-        above = dot(half, lift_t[...])
-        resist = 0.5 + 0.5 * jnp.tanh(2.0 * above)
-        weight = (8.0 * (resist - goal[i].astype(F32))) * (resist * (1.0 - resist))
-        drop = dot(lift_t[...], weight.astype(BF)).astype(BF)
-        pull = (2.0 * dot(drop, lift[...])).astype(BF)
-
-        tot_re = jnp.zeros((FREQ, FREQ), F32)
-        tot_im = jnp.zeros((FREQ, FREQ), F32)
-        for k in range(KERNELS):
-            pulled = field[k] * jnp.concatenate([pull, pull], 0)
-            y = dot(coarse[...], pulled).astype(BF)
-            g = dot(jnp.concatenate([y[:FREQ], y[FREQ:]], 1), coarse_t[...])
-            g_re, g_im = g[:, :FREQ], g[:, FREQ:]
-            h_re, h_im = kern[k, 0], kern[k, 1]
-            tot_re = tot_re + h_re * g_re + h_im * g_im
-            tot_im = tot_im + h_re * g_im - h_im * g_re
-
-        v = dot(jnp.concatenate([tot_re, tot_im], 1).astype(BF), fine[...]).astype(BF)
-        grad = dot(back[...], jnp.concatenate([v[:, :TILE], v[:, TILE:]], 0))
-        level = cls_ref[slot // COLS, slot % COLS]
-        size = 0.5 * steps_ref[level - 1]
-        here = mask[slot]
-        trans = jnp.tanh(0.5 * here)
-        mask[slot] = here - (size * grad) * (1.0 - trans * trans)
-        out_copy(slot).start()
-        return 0
-
-    lax.fori_loop(0, count, tile, 0)
-
-    for s in range(SLOTS):
-        out_copy(s).wait()
+            keep_copy(s).wait()
 
 
 def take_step(cls, steps, mask, target, wide, kernels, tabs):
@@ -211,13 +288,15 @@
             pltpu.SMEM((SLOTS,), jnp.int32),
             pltpu.VMEM((MOST, TILE, TILE), BF),
             pltpu.VMEM((SLOTS, TILE, TILE), F32),
-            pltpu.VMEM((KERNELS, 2 * GRID, GRID), BF),
-            pltpu.VMEM((GRID, GRID), F32),
+            pltpu.VMEM((MOST, TILE, TILE), F32),
+            pltpu.VMEM((LANES, KERNELS, GRID, 2 * GRID), BF),
+            pltpu.VMEM((LANES, GRID, GRID), F32),
             dma((MOST,)),
             dma((SLOTS,)),
+            dma((MOST,)),
             dma((SLOTS,)),
         ],
-        compiler_params=pltpu.CompilerParams(vmem_limit_bytes=32 * 1024 * 1024),
+        compiler_params=pltpu.CompilerParams(vmem_limit_bytes=48 * 1024 * 1024),
         cost_estimate=pl.CostEstimate(
             flops=30_000_000_000, bytes_accessed=40_000_000, transcendentals=3_000_000
         ),

time: 53.8 us -> 38.9 us (0.72)
  the two profiles are of different devices: /device:TPU:33 before, /device:TPU:4 now
where the time goes in v3:
time: 38.9 us; the launch traced here: 38.8 us
  Pallas kernels  38.6 us (99%)
    pallas_call x1, Pallas kernels, take_step(): pl.pallas_call(step_kernel, out_shape=jax.ShapeDtypeStruct((ROWS_HERE, CO...  22.6 us
    pallas_call x1, Pallas kernels, widen(): pl.pallas_call(functools.partial(margin_kernel, n_rows, n_cols), out_shap...  16 us

profile of v3, /device:TPU:4, one launch (start us, length us, event | category | flops | bytes accessed | tf_op | source)
XLA Modules:
  0.0 38.8 jit_solution(9552672305986176239)
XLA Ops:
  0.0 0.0 copy-start.1
  0.0 0.0 copy-start.2
  0.0 0.0 copy-start.3
  0.0 0.0 copy-start.4
  0.0 0.0 copy-start.5
  0.0 0.0 copy-start.6
  0.0 0.0 copy-start.7
  0.1 0.0 copy-start.8
  0.1 0.0 copy-start
  0.1 16.0 %shard_map.127.wide = bf16[1152,2304]{1,0:T(8,128)(2,1)S(1)} custom-call(f32[1024,2048]{1,0:T(8,128)} %mask_hbm.3), custom_call_target="tpu_custom_call" | custom-call | flops 10000000 | bytes 14000000 | tf_op jit(solution)/shard_map/pallas_call | solution.py:434
  16.1 0.0 copy-done.1
  16.1 0.0 copy-done.2
  16.1 0.0 copy-done.3
  16.1 0.0 copy-done.4
  16.1 0.0 copy-done.5
  16.1 0.0 copy-done.6
  16.1 0.0 copy-done.7
  16.1 0.0 copy-done.8
  16.1 0.0 copy-done
  16.2 22.6 %shard_map.128 = f32[1024,2048]{1,0:T(8,128)} custom-call(s32[2,4]{1,0:T(2,128)} %cls_ref.1, f32[3]{0:T(128)} %steps_ref.1, f32[1024,2048]{1,0:T(8,128)} %mask_hbm.3, bf16[1024,2048]{1,0:T(8,128)(2,1)} %target_hbm.1, bf16[1152,2304]{1,0:T(8,128)(2,1)S(1)} %shard_map.127.wide, f32[12,2,128,128]{3,2,1,0:T(8,128)S(1)} %copy-done, ...), custom_call_target="tpu_custom_call" | custom-call | flops 30000001024 | bytes 40000000 | tf_op jit(solution)/shard_map/pallas_call | solution.py:282
Async XLA Ops:
  0.0 16.1 %copy-start.1 = (bf16[256,1024]{1,0:T(8,128)(2,1)S(1)}, bf16[256,1024]{1,0:T(8,128)(2,1)}, u32[]{:S(2)}) copy-start(bf16[256,1024]{1,0:T(8,128)(2,1)} %constant.22.clone.fine) | copy-start | bytes 1572868
  0.0 16.1 %copy-start.2 = (bf16[768,256]{1,0:T(8,128)(2,1)S(1)}, bf16[768,256]{1,0:T(8,128)(2,1)}, u32[]{:S(2)}) copy-start(bf16[768,256]{1,0:T(8,128)(2,1)} %constant.16.clone.spread) | copy-start | bytes 1179652
  0.0 16.1 %copy-start.3 = (bf16[256,640]{1,0:T(8,128)(2,1)S(1)}, bf16[256,640]{1,0:T(8,128)(2,1)}, u32[]{:S(2)}) copy-start(bf16[256,640]{1,0:T(8,128)(2,1)} %constant.17.clone.rows) | copy-start | bytes 983044
  0.0 16.1 %copy-start.4 = (bf16[512,256]{1,0:T(8,128)(2,1)S(1)}, bf16[512,256]{1,0:T(8,128)(2,1)}, u32[]{:S(2)}) copy-start(bf16[512,256]{1,0:T(8,128)(2,1)} %constant.23.clone.back) | copy-start | bytes 786436
  0.0 16.1 %copy-start.5 = (bf16[256,512]{1,0:T(8,128)(2,1)S(1)}, bf16[256,512]{1,0:T(8,128)(2,1)}, u32[]{:S(2)}) copy-start(bf16[256,512]{1,0:T(8,128)(2,1)} %constant.21.clone.lift_t) | copy-start | bytes 786436
  0.0 16.1 %copy-start.6 = (bf16[512,256]{1,0:T(8,128)(2,1)S(1)}, bf16[512,256]{1,0:T(8,128)(2,1)}, u32[]{:S(2)}) copy-start(bf16[512,256]{1,0:T(8,128)(2,1)} %constant.20.clone.lift) | copy-start | bytes 786436
  0.0 16.1 %copy-start.7 = (bf16[512,256]{1,0:T(8,128)(2,1)S(1)}, bf16[512,256]{1,0:T(8,128)(2,1)}, u32[]{:S(2)}) copy-start(bf16[512,256]{1,0:T(8,128)(2,1)} %constant.19.clone.coarse_t) | copy-start | bytes 786436
  0.1 16.1 %copy-start.8 = (bf16[256,512]{1,0:T(8,128)(2,1)S(1)}, bf16[256,512]{1,0:T(8,128)(2,1)}, u32[]{:S(2)}) copy-start(bf16[256,512]{1,0:T(8,128)(2,1)} %constant.18.clone.coarse) | copy-start | bytes 786436
  0.1 16.1 %copy-start = (f32[12,2,128,128]{3,2,1,0:T(8,128)S(1)}, f32[12,2,128,128]{3,2,1,0:T(8,128)}, u32[]{:S(2)}) copy-start(f32[12,2,128,128]{3,2,1,0:T(8,128)} %kern.1) | copy-start | bytes 4718596

commit v4 on v3

--- a/solution.py
+++ b/solution.py
@@ -39,6 +39,8 @@
     cos, sin = waves(PAD, PAD)
     spread = np.zeros((WIDE, 2 * FREQ))
     spread[SIDE - APRON : SIDE + TILE + APRON] = np.concatenate([cos, sin], 0).T
+    ends = [spread[:SIDE], spread[WIDE - SIDE :]]
+    edges = np.stack([np.stack([e, np.roll(e, APRON, 0)]) for e in ends])
     rows = np.concatenate([cos, sin], 0)
     cg, sg = waves(GRID, GRID)
     coarse = np.block([[cg, sg], [-sg, cg]])
@@ -51,20 +53,8 @@
     lift = lift / GRID
     return [
         np.ascontiguousarray(t).astype(ml_dtypes.bfloat16)
-        for t in (spread, rows, coarse, coarse.T, lift, lift.T, fine, back)
+        for t in (spread, edges, rows, coarse, coarse.T, lift, lift.T, fine, back)
     ]
-
-
-TABLE_SHAPES = (
-    (WIDE, 2 * FREQ),
-    (2 * FREQ, PAD),
-    (2 * FREQ, 2 * GRID),
-    (2 * GRID, 2 * FREQ),
-    (TILE, GRID),
-    (GRID, TILE),
-    (2 * FREQ, 2 * TILE),
-    (TILE, 2 * FREQ),
-)
 
 
 def dot(a, b):
@@ -76,9 +66,8 @@
     steps_ref,
     mask_hbm,
     target_hbm,
-    wide,
+    half_spectra,
     kern,
-    spread,
     rows,
     coarse,
     coarse_t,
@@ -157,8 +146,7 @@
         keep()
 
     def spectrum(t):
-        first = dot(wide[pl.ds(t.r, PAD), pl.ds(t.c, WIDE)], spread[...]).astype(BF)
-        blocks = dot(rows[...], first)
+        blocks = dot(rows[...], half_spectra[t.slot % COLS, pl.ds(t.r, PAD), :])
         re = blocks[:FREQ, :FREQ] - blocks[FREQ:, FREQ:]
         im = -(blocks[:FREQ, FREQ:] + blocks[FREQ:, :FREQ])
         t.spec_re = jnp.concatenate([re, re], 1)
@@ -232,7 +220,7 @@
         def __init__(self, i, lane):
             self.i, self.lane = i, lane
             self.slot = slot_ref[i]
-            self.r, self.c = corner(self.slot)
+            self.r = pl.multiple_of(self.slot // COLS * TILE, TILE)
 
     def batch(b, _):
         start = b * LANES
@@ -273,7 +261,7 @@
             keep_copy(s).wait()
 
 
-def take_step(cls, steps, mask, target, wide, kernels, tabs):
+def take_step(cls, steps, mask, target, half_spectra, kernels, tabs):
     hbm = pl.BlockSpec(memory_space=pltpu.HBM)
     vmem = pl.BlockSpec(memory_space=pltpu.VMEM)
     smem = pl.BlockSpec(memory_space=pltpu.SMEM)
@@ -282,7 +270,7 @@
     return pl.pallas_call(
         step_kernel,
         out_shape=jax.ShapeDtypeStruct((ROWS_HERE, COLS_HERE), F32),
-        in_specs=[smem, smem, hbm, hbm, vmem, vmem] + [vmem] * len(TABLE_SHAPES),
+        in_specs=[smem, smem, hbm, hbm, vmem, vmem] + [vmem] * len(tabs),
         out_specs=hbm,
         scratch_shapes=[
             pltpu.SMEM((SLOTS,), jnp.int32),
@@ -305,7 +293,7 @@
         steps,
         here(mask, pltpu.HBM),
         here(target, pltpu.HBM),
-        here(wide, pltpu.VMEM),
+        here(half_spectra, pltpu.VMEM),
         here(kernels, pltpu.VMEM),
         *[here(t, pltpu.VMEM) for t in tabs],
     )
@@ -313,25 +301,37 @@
 
 CORNERS = ((-1, -1), (-1, 1), (1, -1), (1, 1))
 SIDES = ((-1, 0), (1, 0), (0, -1), (0, 1)) + CORNERS
-CHUNK = 128
+CHUNK = 256
 CHUNKS = ROWS_HERE // CHUNK
+HALF = ROWS_HERE // 2
+
+
+def near_transform(trans, spread):
+    pieces = []
+    for c in range(COLS):
+        first, last = c * TILE - SIDE, (c + 1) * TILE + SIDE
+        low, high = max(first, 0), min(last, COLS_HERE)
+        pieces.append(dot(trans[:, low:high], spread[low - first : high - first, :]))
+    return pieces
 
 
 def margin_kernel(
     n_rows,
     n_cols,
     mask_hbm,
-    wide,
-    rows_in,
-    cols_in,
+    spread,
+    edges,
+    out,
+    mask,
     rows_out,
     cols_out,
     corners_out,
-    chunk_in,
-    chunk_out,
-    in_sem,
+    rows_got,
+    cols_got,
+    corners_got,
+    part,
+    strip_sem,
     chunk_sem,
-    store_sem,
     send_sem,
     recv_sem,
 ):
@@ -346,123 +346,146 @@
             barrier, inc=1, device_id=near(dr, dc), device_id_type=pl.DeviceIdType.MESH
         )
 
-    strips = []
+    def load(r, height, c, width, sem):
+        where = (pl.ds(r, height), pl.ds(c, width))
+        return pltpu.make_async_copy(mask_hbm.at[where], mask.at[where], sem)
+
+    inner = ROWS_HERE - 2 * APRON
+    strips = [
+        load(0, APRON, 0, COLS_HERE, strip_sem.at[0]),
+        load(ROWS_HERE - APRON, APRON, 0, COLS_HERE, strip_sem.at[1]),
+        load(APRON, inner, 0, SIDE, strip_sem.at[2]),
+        load(APRON, inner, COLS_HERE - SIDE, SIDE, strip_sem.at[3]),
+    ]
+    chunks = []
+    for n in range(CHUNKS):
+        top = max(n * CHUNK, APRON)
+        height = min((n + 1) * CHUNK, ROWS_HERE - APRON) - top
+        chunks.append(load(top, height, SIDE, COLS_HERE - 2 * SIDE, chunk_sem.at[n]))
+    for copy in strips + chunks:
+        copy.start()
+
+    inside_r = [(row > 0).astype(F32), (row < n_rows - 1).astype(F32)]
+    inside_c = [(col > 0).astype(F32), (col < n_cols - 1).astype(F32)]
+
+    strips[0].wait()
+    strips[1].wait()
+    bands = []
     for side in range(2):
         start = side * (ROWS_HERE - APRON)
-        strips.append(
-            pltpu.make_async_copy(
-                mask_hbm.at[pl.ds(start, APRON), :], rows_in.at[side], in_sem.at[side]
-            )
-        )
+        band = jnp.tanh(0.5 * mask[start : start + APRON, :]) * inside_r[side]
+        bands.append(band.astype(BF))
+        for other in range(2):
+            begin = other * (COLS_HERE - SIDE)
+            cut = band[:, begin : begin + SIDE] * inside_c[other]
+            corners_out[2 * side + other] = cut.astype(BF)
+    for c, piece in enumerate(near_transform(jnp.concatenate(bands, 0), spread)):
+        for side in range(2):
+            rows_out[side, c] = piece[side * APRON : (side + 1) * APRON].astype(BF)
+
+    strips[2].wait()
+    strips[3].wait()
+    left_lanes = lax.broadcasted_iota(jnp.int32, (HALF, SIDE), 1) < APRON
+    for side in range(2):
         start = side * (COLS_HERE - SIDE)
-        strips.append(
-            pltpu.make_async_copy(
-                mask_hbm.at[:, pl.ds(start, SIDE)], cols_in.at[side], in_sem.at[2 + side]
-            )
-        )
-    for copy in strips:
-        copy.start()
-
-    def load(n):
-        return pltpu.make_async_copy(
-            mask_hbm.at[pl.ds(n * CHUNK, CHUNK), :], chunk_in.at[n % 3], chunk_sem.at[n % 3]
-        )
-
-    def store(n):
-        return pltpu.make_async_copy(
-            chunk_out.at[n % 2],
-            wide.at[pl.ds(APRON + n * CHUNK, CHUNK), pl.ds(SIDE, COLS_HERE)],
-            store_sem.at[n % 2],
-        )
-
-    load(0).start()
-    load(1).start()
-
-    inside_r = [(row > 0).astype(F32), (row < n_rows - 1).astype(F32)]
-    inside_c = [(col > 0).astype(F32), (col < n_cols - 1).astype(F32)]
-    for copy in strips:
-        copy.wait()
-    for side in range(2):
-        strip = jnp.tanh(0.5 * rows_in[side]) * inside_r[side]
-        rows_out[side] = strip.astype(BF)
-        for other in range(2):
-            cut = strip[:, :SIDE] if other == 0 else strip[:, COLS_HERE - SIDE :]
-            corners_out[2 * side + other] = (cut * inside_c[other]).astype(BF)
-        cols_out[side] = (jnp.tanh(0.5 * cols_in[side]) * inside_c[side]).astype(BF)
-
+        band = jnp.tanh(0.5 * mask[:, start : start + SIDE]) * inside_c[side]
+        upper, lower = band[:HALF], pltpu.roll(band[HALF:], APRON, 1)
+        if side == 1:
+            upper, lower = lower, upper
+        cols_out[side] = jnp.where(left_lanes, upper, lower).astype(BF)
+
+    sources = [rows_out.at[0], rows_out.at[1], cols_out.at[0], cols_out.at[1]]
+    places = [rows_got.at[1], rows_got.at[0], cols_got.at[1], cols_got.at[0]]
+    for n in range(len(CORNERS)):
+        sources.append(corners_out.at[n])
+        places.append(corners_got.at[len(CORNERS) - 1 - n])
+    sends = [
+        pltpu.make_async_remote_copy(
+            src_ref=sources[n],
+            dst_ref=places[n],
+            send_sem=send_sem.at[n],
+            recv_sem=recv_sem.at[n],
+            device_id=near(dr, dc),
+            device_id_type=pl.DeviceIdType.MESH,
+        )
+        for n, (dr, dc) in enumerate(SIDES)
+    ]
     pl.semaphore_wait(barrier, len(SIDES))
-
-    row_place = {-1: pl.ds(APRON + ROWS_HERE, APRON), 1: pl.ds(0, APRON), 0: pl.ds(APRON, ROWS_HERE)}
-    col_place = {-1: pl.ds(SIDE + COLS_HERE, SIDE), 1: pl.ds(0, SIDE), 0: pl.ds(SIDE, COLS_HERE)}
-    sources = [
-        rows_out.at[0],
-        rows_out.at[1],
-        cols_out.at[0],
-        cols_out.at[1],
-    ] + [corners_out.at[n] for n in range(4)]
-    sends = []
-    for n, (dr, dc) in enumerate(SIDES):
-        sends.append(
-            pltpu.make_async_remote_copy(
-                src_ref=sources[n],
-                dst_ref=wide.at[row_place[dr], col_place[dc]],
-                send_sem=send_sem.at[n],
-                recv_sem=recv_sem.at[n],
-                device_id=near(dr, dc),
-                device_id_type=pl.DeviceIdType.MESH,
-            )
-        )
     for send in sends:
         send.start()
 
     for n in range(CHUNKS):
-        if n + 2 < CHUNKS:
-            load(n + 2).start()
-        load(n).wait()
-        if n >= 2:
-            store(n - 2).wait()
-        chunk_out[n % 2] = jnp.tanh(0.5 * chunk_in[n % 3]).astype(BF)
-        store(n).start()
-    store(CHUNKS - 2).wait()
-    store(CHUNKS - 1).wait()
-    for send in sends:
+        chunks[n].wait()
+        here = slice(n * CHUNK, (n + 1) * CHUNK)
+        pieces = near_transform(jnp.tanh(0.5 * mask[here, :]).astype(BF), spread)
+        part[0, here] = pieces[0]
+        part[1, here] = pieces[-1]
+        for c in range(1, COLS - 1):
+            out[c, APRON + n * CHUNK : APRON + (n + 1) * CHUNK] = pieces[c].astype(BF)
+
+    sends[2].wait()
+    sends[3].wait()
+    for side, c in ((0, 0), (1, COLS - 1)):
+        for h in range(2):
+            here = slice(h * HALF, (h + 1) * HALF)
+            whole = part[side, here] + dot(cols_got[side], edges[side, h])
+            out[c, APRON + h * HALF : APRON + (h + 1) * HALF] = whole.astype(BF)
+    sends[0].wait()
+    sends[1].wait()
+    for send in sends[4:]:
         send.wait()
-
-
-def widen(mask, n_rows, n_cols):
+    for side in range(2):
+        start = side * (APRON + ROWS_HERE)
+        for c in range(COLS):
+            value = rows_got[side, c]
+            other = {0: 0, COLS - 1: 1}.get(c)
+            if other is not None:
+                corner = dot(corners_got[2 * side + other], edges[other, 0])
+                value = (value.astype(F32) + corner).astype(BF)
+            out[c, start : start + APRON] = value
+
+
+def half_transform(mask, spread, edges, n_rows, n_cols):
+    vmem = pl.BlockSpec(memory_space=pltpu.VMEM)
     dma = pltpu.SemaphoreType.DMA
+    here = pltpu.with_memory_space_constraint
+    rows_shape = (2, COLS, APRON, 2 * FREQ)
+    cols_shape = (2, HALF, SIDE)
+    corners_shape = (len(CORNERS), APRON, SIDE)
     return pl.pallas_call(
         functools.partial(margin_kernel, n_rows, n_cols),
-        out_shape=pltpu.VMEM((ROWS_HERE + 2 * APRON, COLS_HERE + 2 * SIDE), BF),
-        in_specs=[pl.BlockSpec(memory_space=pltpu.HBM)],
-        out_specs=pl.BlockSpec(memory_space=pltpu.VMEM),
+        out_shape=pltpu.VMEM((COLS, ROWS_HERE + 2 * APRON, 2 * FREQ), BF),
+        in_specs=[pl.BlockSpec(memory_space=pltpu.HBM), vmem, vmem],
+        out_specs=vmem,
         scratch_shapes=[
-            pltpu.VMEM((2, APRON, COLS_HERE), F32),
-            pltpu.VMEM((2, ROWS_HERE, SIDE), F32),
-            pltpu.VMEM((2, APRON, COLS_HERE), BF),
-            pltpu.VMEM((2, ROWS_HERE, SIDE), BF),
-            pltpu.VMEM((4, APRON, SIDE), BF),
-            pltpu.VMEM((3, CHUNK, COLS_HERE), F32),
-            pltpu.VMEM((2, CHUNK, COLS_HERE), BF),
+            pltpu.VMEM((ROWS_HERE, COLS_HERE), F32),
+            pltpu.VMEM(rows_shape, BF),
+            pltpu.VMEM(cols_shape, BF),
+            pltpu.VMEM(corners_shape, BF),
+            pltpu.VMEM(rows_shape, BF),
+            pltpu.VMEM(cols_shape, BF),
+            pltpu.VMEM(corners_shape, BF),
+            pltpu.VMEM((2, ROWS_HERE, 2 * FREQ), F32),
             dma((4,)),
-            dma((3,)),
-            dma((2,)),
+            dma((CHUNKS,)),
             dma((len(SIDES),)),
             dma((len(SIDES),)),
         ],
         compiler_params=pltpu.CompilerParams(
-            collective_id=0, has_side_effects=True, vmem_limit_bytes=32 * 1024 * 1024
+            collective_id=0, has_side_effects=True, vmem_limit_bytes=40 * 1024 * 1024
         ),
         cost_estimate=pl.CostEstimate(
-            flops=10_000_000, bytes_accessed=14_000_000, transcendentals=2_000_000
+            flops=2_000_000_000, bytes_accessed=10_000_000, transcendentals=2_000_000
         ),
-    )(pltpu.with_memory_space_constraint(mask, pltpu.HBM))
+    )(here(mask, pltpu.HBM), here(spread, pltpu.VMEM), here(edges, pltpu.VMEM))
 
 
 def body(mask_level, target, kernels, step_sizes, density_class, work_list):
-    wide = widen(mask_level, lax.axis_size("trow"), lax.axis_size("tcol"))
-    tabs = [jnp.asarray(t) for t in tables()]
-    return take_step(density_class, step_sizes, mask_level, target, wide, kernels, tabs)
+    spread, edges, *tabs = [jnp.asarray(t) for t in tables()]
+    half_spectra = half_transform(
+        mask_level, spread, edges, lax.axis_size("trow"), lax.axis_size("tcol")
+    )
+    return take_step(density_class, step_sizes, mask_level, target, half_spectra, kernels, tabs)
 
 
 def solution(mesh):

time: 38.9 us -> 38.4 us (0.987)
  the two profiles are of different devices: /device:TPU:4 before, /device:TPU:1 now
where the time goes in v4:
time: 38.4 us; the launch traced here: 38.2 us
  Pallas kernels  35.9 us (93%)
  local copies, waits for them, and re-layouts  2 us (5%)
    pallas_call x1, Pallas kernels, take_step(): pl.pallas_call(step_kernel, out_shape=jax.ShapeDtypeStruct((ROWS_HERE, CO...  21.6 us
    pallas_call x1, Pallas kernels, half_transform(): pl.pallas_call(functools.partial(margin_kernel, n_rows, n_cols), out_shap...  14.3 us
    unnamed x24, local copies, waits for them, and re-layouts  2 us

profile of v4, /device:TPU:1, one launch (start us, length us, event | category | flops | bytes accessed | tf_op | source)
XLA Modules:
  0.0 38.2 jit_solution(17551644863642615604)
XLA Ops:
  0.0 0.0 copy-start
  0.0 1.0 %copy-done = bf16[768,256]{1,0:T(8,128)(2,1)S(1)} copy-done((bf16[768,256]{1,0:T(8,128)(2,1)S(1)}, bf16[768,256]{1,0:T(8,128)(2,1)}, u32[]{:S(2)}) %copy-start) | copy-done | bytes 393240
  1.0 0.0 copy-start.1
  1.0 0.9 %copy-done.1 = bf16[2,2,128,256]{3,2,1,0:T(8,128)(2,1)S(1)} copy-done((bf16[2,2,128,256]{3,2,1,0:T(8,128)(2,1)S(1)}, bf16[2,2,128,256]{3,2,1,0:T(8,128)(2,1)}, u32[]{:S(2)}) %copy-start.1) | copy-done | bytes 262168
  1.9 0.0 copy-start.2
  1.9 0.0 copy-start.3
  2.0 0.0 copy-start.4
  2.0 0.0 copy-start.5
  2.0 0.0 copy-start.6
  2.0 0.0 copy-start.7
  2.0 0.0 copy-start.8
  2.0 0.0 copy-start.9
  2.0 0.0 copy-start.10
  2.0 0.0 copy-start.11
  2.0 14.3 %shard_map.136.half_spectra = bf16[4,1152,256]{2,1,0:T(8,128)(2,1)S(1)} custom-call(f32[1024,2048]{1,0:T(8,128)} %mask_hbm.3, bf16[768,256]{1,0:T(8,128)(2,1)S(1)} %copy-done, bf16[2,2,128,256]{3,2,1,0:T(8,128)(2,1)S(1)} %copy-done.1), custom_call_target="tpu_custom_call" | custom-call | flops 2000000000 | bytes 10000000 | tf_op jit(solution)/shard_map/pallas_call | solution.py:455
  16.3 0.0 copy-done.2
  16.3 0.0 copy-done.3
  16.4 0.0 copy-done.4
  16.4 0.0 copy-done.5
  16.4 0.0 copy-done.6
  16.4 0.0 copy-done.7
  16.4 0.0 copy-done.8
  16.4 0.0 copy-done.9
  16.4 0.0 copy-done.10
  16.4 0.0 copy-done.11
  16.4 21.6 %shard_map.137 = f32[1024,2048]{1,0:T(8,128)} custom-call(s32[2,4]{1,0:T(2,128)S(1)} %copy-done.3, f32[3]{0:T(128)S(1)} %copy-done.4, f32[1024,2048]{1,0:T(8,128)} %mask_hbm.3, bf16[1024,2048]{1,0:T(8,128)(2,1)} %target_hbm.1, bf16[4,1152,256]{2,1,0:T(8,128)(2,1)S(1)} %shard_map.136.half_spectra, f32[12,2,128,128]{3,2,1,0:T(8,128)S(1)} %copy-done.2, ...), custom_call_target="tpu_custom_call" | custom-call | flops 30000001024 | bytes 40000000 | tf_op jit(solution)/shard_map/pallas_call | solution.py:270
Async XLA Ops:
  0.0 1.0 %copy-start = (bf16[768,256]{1,0:T(8,128)(2,1)S(1)}, bf16[768,256]{1,0:T(8,128)(2,1)}, u32[]{:S(2)}) copy-start(bf16[768,256]{1,0:T(8,128)(2,1)} %constant.18.clone.spread) | copy-start | bytes 1179652
  1.0 0.9 %copy-start.1 = (bf16[2,2,128,256]{3,2,1,0:T(8,128)(2,1)S(1)}, bf16[2,2,128,256]{3,2,1,0:T(8,128)(2,1)}, u32[]{:S(2)}) copy-start(bf16[2,2,128,256]{3,2,1,0:T(8,128)(2,1)} %constant.19.clone.edges) | copy-start | bytes 786436
  1.9 14.4 %copy-start.2 = (f32[12,2,128,128]{3,2,1,0:T(8,128)S(1)}, f32[12,2,128,128]{3,2,1,0:T(8,128)}, u32[]{:S(2)}) copy-start(f32[12,2,128,128]{3,2,1,0:T(8,128)} %kern.1) | copy-start | bytes 4718596
  1.9 14.4 %copy-start.3 = (s32[2,4]{1,0:T(2,128)S(1)}, s32[2,4]{1,0:T(2,128)}, u32[]{:S(2)}) copy-start(s32[2,4]{1,0:T(2,128)} %cls_ref.1) | copy-start | bytes 100
  2.0 14.4 %copy-start.4 = (f32[3]{0:T(128)S(1)}, f32[3]{0:T(128)}, u32[]{:S(2)}) copy-start(f32[3]{0:T(128)} %steps_ref.1) | copy-start | bytes 40
  2.0 14.4 %copy-start.5 = (bf16[256,1024]{1,0:T(8,128)(2,1)S(1)}, bf16[256,1024]{1,0:T(8,128)(2,1)}, u32[]{:S(2)}) copy-start(bf16[256,1024]{1,0:T(8,128)(2,1)} %constant.25.clone.fine) | copy-start | bytes 1572868
  2.0 14.4 %copy-start.6 = (bf16[256,640]{1,0:T(8,128)(2,1)S(1)}, bf16[256,640]{1,0:T(8,128)(2,1)}, u32[]{:S(2)}) copy-start(bf16[256,640]{1,0:T(8,128)(2,1)} %constant.20.clone.rows) | copy-start | bytes 983044
  2.0 14.4 %copy-start.7 = (bf16[512,256]{1,0:T(8,128)(2,1)S(1)}, bf16[512,256]{1,0:T(8,128)(2,1)}, u32[]{:S(2)}) copy-start(bf16[512,256]{1,0:T(8,128)(2,1)} %constant.26.clone.back) | copy-start | bytes 786436
  2.0 14.4 %copy-start.8 = (bf16[256,512]{1,0:T(8,128)(2,1)S(1)}, bf16[256,512]{1,0:T(8,128)(2,1)}, u32[]{:S(2)}) copy-start(bf16[256,512]{1,0:T(8,128)(2,1)} %constant.24.clone.lift_t) | copy-start | bytes 786436
  2.0 14.4 %copy-start.9 = (bf16[512,256]{1,0:T(8,128)(2,1)S(1)}, bf16[512,256]{1,0:T(8,128)(2,1)}, u32[]{:S(2)}) copy-start(bf16[512,256]{1,0:T(8,128)(2,1)} %constant.23.clone.lift) | copy-start | bytes 786436
  2.0 14.4 %copy-start.10 = (bf16[512,256]{1,0:T(8,128)(2,1)S(1)}, bf16[512,256]{1,0:T(8,128)(2,1)}, u32[]{:S(2)}) copy-start(bf16[512,256]{1,0:T(8,128)(2,1)} %constant.22.clone.coarse_t) | copy-start | bytes 786436
  2.0 14.4 %copy-start.11 = (bf16[256,512]{1,0:T(8,128)(2,1)S(1)}, bf16[256,512]{1,0:T(8,128)(2,1)}, u32[]{:S(2)}) copy-start(bf16[256,512]{1,0:T(8,128)(2,1)} %constant.21.clone.coarse) | copy-start | bytes 786436

commit v5 on v4

--- a/solution.py
+++ b/solution.py
@@ -16,8 +16,8 @@
 KERNELS = 12
 MOST = 4
 SLOTS = 8
-GROUP = 12
 LANES = 2
+PART = 512
 COLS = 4
 GRID = 256
 SIDE = 128
@@ -149,31 +149,30 @@
         blocks = dot(rows[...], half_spectra[t.slot % COLS, pl.ds(t.r, PAD), :])
         re = blocks[:FREQ, :FREQ] - blocks[FREQ:, FREQ:]
         im = -(blocks[:FREQ, FREQ:] + blocks[FREQ:, :FREQ])
-        t.spec_re = jnp.concatenate([re, re], 1)
-        t.spec_im = jnp.concatenate([im, im], 1)
-
-    def forward(t, k):
+        t.spec_re, t.spec_im = re, im
+
+    def kernel_lanes(part):
+        return jnp.concatenate([kern[k, part] for k in range(KERNELS)], 1)
+
+    def forward(t, _):
+        h_re, h_im = kernel_lanes(0), kernel_lanes(1)
+        re = jnp.concatenate([t.spec_re] * KERNELS, 1)
+        im = jnp.concatenate([t.spec_im] * KERNELS, 1)
+        z_re = (h_re * re - h_im * im).astype(BF)
+        z_im = (h_re * im + h_im * re).astype(BF)
+        w = dot(coarse_t[...], jnp.concatenate([z_re, z_im], 0)).astype(BF)
         parts = []
-        for p in range(k, k + GROUP, 2):
-            h_re = jnp.concatenate([kern[p, 0], kern[p + 1, 0]], 1)
-            h_im = jnp.concatenate([kern[p, 1], kern[p + 1, 1]], 1)
-            z_re = (h_re * t.spec_re - h_im * t.spec_im).astype(BF)
-            z_im = (h_re * t.spec_im + h_im * t.spec_re).astype(BF)
-            w = dot(coarse_t[...], jnp.concatenate([z_re, z_im], 0)).astype(BF)
-            for n in range(2):
-                cut = w[:, n * FREQ : (n + 1) * FREQ]
-                parts.append(jnp.concatenate([cut[:GRID], cut[GRID:]], 1))
+        for k in range(KERNELS):
+            cut = w[:, k * FREQ : (k + 1) * FREQ]
+            parts.append(jnp.concatenate([cut[:GRID], cut[GRID:]], 1))
         f = dot(jnp.concatenate(parts, 0), coarse[...])
         total = None
-        for n in range(GROUP):
-            one = f[n * GRID : (n + 1) * GRID]
-            field[t.lane, k + n] = one.astype(BF)
+        for k in range(KERNELS):
+            one = f[k * GRID : (k + 1) * GRID]
+            field[t.lane, k] = one.astype(BF)
             square = one[:, :GRID] * one[:, :GRID] + one[:, GRID:] * one[:, GRID:]
             total = square if total is None else total + square
-        if k == 0:
-            inten[t.lane] = total - 1.0
-        else:
-            inten[t.lane] += total
+        inten[t.lane] = total - 1.0
 
     def resist(t):
         half = dot(lift[...], (2.0 * inten[t.lane]).astype(BF)).astype(BF)
@@ -182,34 +181,52 @@
         drop = dot(lift_t[...], weight.astype(BF)).astype(BF)
         pull = (2.0 * dot(drop, lift[...])).astype(BF)
         t.pull = jnp.concatenate([pull, pull], 1)
-        t.tot_re = jnp.zeros((FREQ, 2 * FREQ), F32)
-        t.tot_im = jnp.zeros((FREQ, 2 * FREQ), F32)
-
-    def adjoint(t, k):
-        pulled = jnp.concatenate([field[t.lane, k + n] * t.pull for n in range(GROUP)], 0)
-        x = dot(pulled, coarse_t[...]).astype(BF)
-        for p in range(0, GROUP, 2):
-            a = x[p * GRID : (p + 1) * GRID]
-            b = x[(p + 1) * GRID : (p + 2) * GRID]
-            pair = jnp.concatenate(
-                [
-                    jnp.concatenate([a[:, :FREQ], b[:, :FREQ]], 1),
-                    jnp.concatenate([a[:, FREQ:], b[:, FREQ:]], 1),
-                ],
-                0,
-            )
-            g = dot(coarse[...], pair)
-            g_re, g_im = g[:FREQ], g[FREQ:]
-            h_re = jnp.concatenate([kern[k + p, 0], kern[k + p + 1, 0]], 1)
-            h_im = jnp.concatenate([kern[k + p, 1], kern[k + p + 1, 1]], 1)
-            t.tot_re = t.tot_re + h_re * g_re + h_im * g_im
-            t.tot_im = t.tot_im + h_re * g_im - h_im * g_re
+
+    def adjoint(t, _):
+        pulled = jnp.concatenate([field[t.lane, k] * t.pull for k in range(KERNELS)], 0)
+        x = jnp.concatenate(
+            [
+                dot(pulled[m : m + PART], coarse_t[...]).astype(BF)
+                for m in range(0, KERNELS * GRID, PART)
+            ],
+            0,
+        )
+        wide = jnp.concatenate(
+            [
+                jnp.concatenate(
+                    [
+                        x[k * GRID : (k + 1) * GRID, part * FREQ : (part + 1) * FREQ]
+                        for k in range(KERNELS)
+                    ],
+                    1,
+                )
+                for part in range(2)
+            ],
+            0,
+        )
+        g = jnp.concatenate(
+            [
+                dot(coarse[...], wide[:, m : m + PART])
+                for m in range(0, KERNELS * FREQ, PART)
+            ],
+            1,
+        )
+        tot_re = tot_im = None
+        for k in range(KERNELS):
+            cut = g[:, k * FREQ : (k + 1) * FREQ]
+            g_re, g_im = cut[:FREQ], cut[FREQ:]
+            h_re, h_im = kern[k, 0], kern[k, 1]
+            one_re = h_re * g_re + h_im * g_im
+            one_im = h_re * g_im - h_im * g_re
+            tot_re = one_re if k == 0 else tot_re + one_re
+            tot_im = one_im if k == 0 else tot_im + one_im
+        t.tot_re, t.tot_im = tot_re, tot_im
 
     def finish(t):
         level = cls_ref[t.slot // COLS, t.slot % COLS]
         size = 0.5 * steps_ref[level - 1]
-        tot_re = size * (t.tot_re[:, :FREQ] + t.tot_re[:, FREQ:])
-        tot_im = size * (t.tot_im[:, :FREQ] + t.tot_im[:, FREQ:])
+        tot_re = size * t.tot_re
+        tot_im = size * t.tot_im
         v = dot(jnp.concatenate([tot_re, tot_im], 1).astype(BF), fine[...]).astype(BF)
         grad = dot(back[...], jnp.concatenate([v[:, :TILE], v[:, TILE:]], 0))
         here = mask[t.slot]
@@ -227,9 +244,8 @@
         tiles = [Tile(jnp.minimum(start + n, count - 1), n) for n in range(LANES)]
         for t in tiles:
             spectrum(t)
-        for k in range(0, KERNELS, GROUP):
-            for t in tiles:
-                forward(t, k)
+        for t in tiles:
+            forward(t, 0)
 
         @pl.when(b == 0)
         def _():
@@ -238,9 +254,8 @@
 
         for t in tiles:
             resist(t)
-        for k in range(0, KERNELS, GROUP):
-            for t in tiles:
-                adjoint(t, k)
+        for t in tiles:
+            adjoint(t, 0)
         for t in tiles:
             finish(t)
         for n in range(LANES):
@@ -319,10 +334,12 @@
     n_rows,
     n_cols,
     mask_hbm,
+    spread_hbm,
+    edges_hbm,
+    out,
+    mask,
     spread,
     edges,
-    out,
-    mask,
     rows_out,
     cols_out,
     corners_out,
@@ -331,6 +348,7 @@
     corners_got,
     part,
     strip_sem,
+    table_sem,
     chunk_sem,
     send_sem,
     recv_sem,
@@ -362,11 +380,21 @@
         top = max(n * CHUNK, APRON)
         height = min((n + 1) * CHUNK, ROWS_HERE - APRON) - top
         chunks.append(load(top, height, SIDE, COLS_HERE - 2 * SIDE, chunk_sem.at[n]))
-    for copy in strips + chunks:
+    near_table = pltpu.make_async_copy(spread_hbm, spread, table_sem.at[0])
+    edge_table = pltpu.make_async_copy(edges_hbm, edges, table_sem.at[1])
+    for copy in strips[:2] + [near_table] + strips[2:] + chunks[:1] + [edge_table] + chunks[1:]:
         copy.start()
 
     inside_r = [(row > 0).astype(F32), (row < n_rows - 1).astype(F32)]
     inside_c = [(col > 0).astype(F32), (col < n_cols - 1).astype(F32)]
+
+    def packed(band, side):
+        half = band.shape[0] // 2
+        upper, lower = band[:half], pltpu.roll(band[half:], APRON, 1)
+        if side == 1:
+            upper, lower = lower, upper
+        lane = lax.broadcasted_iota(jnp.int32, (half, SIDE), 1)
+        return jnp.where(lane < APRON, upper, lower).astype(BF)
 
     strips[0].wait()
     strips[1].wait()
@@ -378,21 +406,11 @@
         for other in range(2):
             begin = other * (COLS_HERE - SIDE)
             cut = band[:, begin : begin + SIDE] * inside_c[other]
-            corners_out[2 * side + other] = cut.astype(BF)
+            corners_out[2 * side + other] = packed(cut, other)
+    near_table.wait()
     for c, piece in enumerate(near_transform(jnp.concatenate(bands, 0), spread)):
         for side in range(2):
             rows_out[side, c] = piece[side * APRON : (side + 1) * APRON].astype(BF)
-
-    strips[2].wait()
-    strips[3].wait()
-    left_lanes = lax.broadcasted_iota(jnp.int32, (HALF, SIDE), 1) < APRON
-    for side in range(2):
-        start = side * (COLS_HERE - SIDE)
-        band = jnp.tanh(0.5 * mask[:, start : start + SIDE]) * inside_c[side]
-        upper, lower = band[:HALF], pltpu.roll(band[HALF:], APRON, 1)
-        if side == 1:
-            upper, lower = lower, upper
-        cols_out[side] = jnp.where(left_lanes, upper, lower).astype(BF)
 
     sources = [rows_out.at[0], rows_out.at[1], cols_out.at[0], cols_out.at[1]]
     places = [rows_got.at[1], rows_got.at[0], cols_got.at[1], cols_got.at[0]]
@@ -411,7 +429,16 @@
         for n, (dr, dc) in enumerate(SIDES)
     ]
     pl.semaphore_wait(barrier, len(SIDES))
-    for send in sends:
+    for send in sends[:2] + sends[4:]:
+        send.start()
+
+    strips[2].wait()
+    strips[3].wait()
+    for side in range(2):
+        start = side * (COLS_HERE - SIDE)
+        band = jnp.tanh(0.5 * mask[:, start : start + SIDE]) * inside_c[side]
+        cols_out[side] = packed(band, side)
+    for send in sends[2:4]:
         send.start()
 
     for n in range(CHUNKS):
@@ -423,6 +450,7 @@
         for c in range(1, COLS - 1):
             out[c, APRON + n * CHUNK : APRON + (n + 1) * CHUNK] = pieces[c].astype(BF)
 
+    edge_table.wait()
     sends[2].wait()
     sends[3].wait()
     for side, c in ((0, 0), (1, COLS - 1)):
@@ -440,7 +468,9 @@
             value = rows_got[side, c]
             other = {0: 0, COLS - 1: 1}.get(c)
             if other is not None:
-                corner = dot(corners_got[2 * side + other], edges[other, 0])
+                got = corners_got[2 * side + other]
+                corner = [dot(got, edges[other, h]) for h in range(2)]
+                corner = jnp.concatenate(corner, 0)
                 value = (value.astype(F32) + corner).astype(BF)
             out[c, start : start + APRON] = value
 
@@ -451,14 +481,16 @@
     here = pltpu.with_memory_space_constraint
     rows_shape = (2, COLS, APRON, 2 * FREQ)
     cols_shape = (2, HALF, SIDE)
-    corners_shape = (len(CORNERS), APRON, SIDE)
+    corners_shape = (len(CORNERS), APRON // 2, SIDE)
     return pl.pallas_call(
         functools.partial(margin_kernel, n_rows, n_cols),
         out_shape=pltpu.VMEM((COLS, ROWS_HERE + 2 * APRON, 2 * FREQ), BF),
-        in_specs=[pl.BlockSpec(memory_space=pltpu.HBM), vmem, vmem],
+        in_specs=[pl.BlockSpec(memory_space=pltpu.HBM)] * 3,
         out_specs=vmem,
         scratch_shapes=[
             pltpu.VMEM((ROWS_HERE, COLS_HERE), F32),
+            pltpu.VMEM((WIDE, 2 * FREQ), BF),
+            pltpu.VMEM((2, 2, SIDE, 2 * FREQ), BF),
             pltpu.VMEM(rows_shape, BF),
             pltpu.VMEM(cols_shape, BF),
             pltpu.VMEM(corners_shape, BF),
@@ -467,6 +499,7 @@
             pltpu.VMEM(corners_shape, BF),
             pltpu.VMEM((2, ROWS_HERE, 2 * FREQ), F32),
             dma((4,)),
+            dma((2,)),
             dma((CHUNKS,)),
             dma((len(SIDES),)),
             dma((len(SIDES),)),
@@ -477,7 +510,7 @@
         cost_estimate=pl.CostEstimate(
             flops=2_000_000_000, bytes_accessed=10_000_000, transcendentals=2_000_000
         ),
-    )(here(mask, pltpu.HBM), here(spread, pltpu.VMEM), here(edges, pltpu.VMEM))
+    )(*[here(a, pltpu.HBM) for a in (mask, spread, edges)])
 
 
 def body(mask_level, target, kernels, step_sizes, density_class, work_list):

time: 38.4 us -> 33.1 us (0.86)
  the two profiles are of different devices: /device:TPU:1 before, /device:TPU:6 now
where the time goes in v5:
time: 33.1 us; the launch traced here: 33 us
  Pallas kernels  32.8 us (99%)
    pallas_call x1, Pallas kernels, take_step(): pl.pallas_call(step_kernel, out_shape=jax.ShapeDtypeStruct((ROWS_HERE, CO...  18.9 us
    pallas_call x1, Pallas kernels, half_transform(): pl.pallas_call(functools.partial(margin_kernel, n_rows, n_cols), out_shap...  13.9 us

profile of v5, /device:TPU:6, one launch (start us, length us, event | category | flops | bytes accessed | tf_op | source)
XLA Modules:
  0.0 33.0 jit_solution(1501634571010321426)
XLA Ops:
  0.0 0.0 copy-start.3
  0.0 0.0 copy-start.4
  0.0 0.0 copy-start.5
  0.0 0.0 copy-start.6
  0.0 0.0 copy-start.7
  0.0 0.0 copy-start.8
  0.0 0.0 copy-start.9
  0.1 0.0 copy-start.1
  0.1 0.0 copy-start.2
  0.1 0.0 copy-start
  0.1 13.9 %shard_map.136.half_spectra = bf16[4,1152,256]{2,1,0:T(8,128)(2,1)S(1)} custom-call(f32[1024,2048]{1,0:T(8,128)} %mask_hbm.3, bf16[768,256]{1,0:T(8,128)(2,1)} %constant.18.clone.spread_hbm, bf16[2,2,128,256]{3,2,1,0:T(8,128)(2,1)} %constant.19.clone.edges_hbm), custom_call_target="tpu_custom_call" | custom-call | flops 2000000000 | bytes 10000000 | tf_op jit(solution)/shard_map/pallas_call | solution.py:485
  14.0 0.0 copy-done.3
  14.1 0.0 copy-done.4
  14.1 0.0 copy-done.5
  14.1 0.0 copy-done.6
  14.1 0.0 copy-done.7
  14.1 0.0 copy-done.8
  14.1 0.0 copy-done.9
  14.1 0.0 copy-done.1
  14.1 0.0 copy-done.2
  14.1 0.0 copy-done
  14.1 18.9 %shard_map.137 = f32[1024,2048]{1,0:T(8,128)} custom-call(s32[2,4]{1,0:T(2,128)S(1)} %copy-done.1, f32[3]{0:T(128)S(1)} %copy-done.2, f32[1024,2048]{1,0:T(8,128)} %mask_hbm.3, bf16[1024,2048]{1,0:T(8,128)(2,1)} %target_hbm.1, bf16[4,1152,256]{2,1,0:T(8,128)(2,1)S(1)} %shard_map.136.half_spectra, f32[12,2,128,128]{3,2,1,0:T(8,128)S(1)} %copy-done, ...), custom_call_target="tpu_custom_call" | custom-call | flops 30000001024 | bytes 40000000 | tf_op jit(solution)/shard_map/pallas_call | solution.py:285
Async XLA Ops:
  0.0 14.0 %copy-start.3 = (bf16[256,1024]{1,0:T(8,128)(2,1)S(1)}, bf16[256,1024]{1,0:T(8,128)(2,1)}, u32[]{:S(2)}) copy-start(bf16[256,1024]{1,0:T(8,128)(2,1)} %constant.25.clone.fine) | copy-start | bytes 1572868
  0.0 14.1 %copy-start.4 = (bf16[256,640]{1,0:T(8,128)(2,1)S(1)}, bf16[256,640]{1,0:T(8,128)(2,1)}, u32[]{:S(2)}) copy-start(bf16[256,640]{1,0:T(8,128)(2,1)} %constant.20.clone.rows) | copy-start | bytes 983044
  0.0 14.1 %copy-start.5 = (bf16[512,256]{1,0:T(8,128)(2,1)S(1)}, bf16[512,256]{1,0:T(8,128)(2,1)}, u32[]{:S(2)}) copy-start(bf16[512,256]{1,0:T(8,128)(2,1)} %constant.26.clone.back) | copy-start | bytes 786436
  0.0 14.1 %copy-start.6 = (bf16[256,512]{1,0:T(8,128)(2,1)S(1)}, bf16[256,512]{1,0:T(8,128)(2,1)}, u32[]{:S(2)}) copy-start(bf16[256,512]{1,0:T(8,128)(2,1)} %constant.24.clone.lift_t) | copy-start | bytes 786436
  0.0 14.1 %copy-start.7 = (bf16[512,256]{1,0:T(8,128)(2,1)S(1)}, bf16[512,256]{1,0:T(8,128)(2,1)}, u32[]{:S(2)}) copy-start(bf16[512,256]{1,0:T(8,128)(2,1)} %constant.23.clone.lift) | copy-start | bytes 786436
  0.0 14.1 %copy-start.8 = (bf16[512,256]{1,0:T(8,128)(2,1)S(1)}, bf16[512,256]{1,0:T(8,128)(2,1)}, u32[]{:S(2)}) copy-start(bf16[512,256]{1,0:T(8,128)(2,1)} %constant.22.clone.coarse_t) | copy-start | bytes 786436
  0.0 14.1 %copy-start.9 = (bf16[256,512]{1,0:T(8,128)(2,1)S(1)}, bf16[256,512]{1,0:T(8,128)(2,1)}, u32[]{:S(2)}) copy-start(bf16[256,512]{1,0:T(8,128)(2,1)} %constant.21.clone.coarse) | copy-start | bytes 786436
  0.1 14.1 %copy-start.1 = (s32[2,4]{1,0:T(2,128)S(1)}, s32[2,4]{1,0:T(2,128)}, u32[]{:S(2)}) copy-start(s32[2,4]{1,0:T(2,128)} %cls_ref.1) | copy-start | bytes 100
  0.1 14.1 %copy-start.2 = (f32[3]{0:T(128)S(1)}, f32[3]{0:T(128)}, u32[]{:S(2)}) copy-start(f32[3]{0:T(128)} %steps_ref.1) | copy-start | bytes 40
  0.1 14.1 %copy-start = (f32[12,2,128,128]{3,2,1,0:T(8,128)S(1)}, f32[12,2,128,128]{3,2,1,0:T(8,128)}, u32[]{:S(2)}) copy-start(f32[12,2,128,128]{3,2,1,0:T(8,128)} %kern.1) | copy-start | bytes 4718596

commit v6 on v5

--- a/solution.py
+++ b/solution.py
@@ -42,6 +42,14 @@
     ends = [spread[:SIDE], spread[WIDE - SIDE :]]
     edges = np.stack([np.stack([e, np.roll(e, APRON, 0)]) for e in ends])
     rows = np.concatenate([cos, sin], 0)
+    half = FREQ // 2
+    mirror = np.zeros((2 * FREQ, 2 * FREQ))
+    for n in range(half):
+        mirror[n, n] = mirror[half + n, FREQ + n] = 1.0
+        if n:
+            mirror[n, FREQ - n] = 1.0
+            mirror[half + n, 2 * FREQ - n] = -1.0
+    mirror[FREQ:, half] = 1.0
     cg, sg = waves(GRID, GRID)
     coarse = np.block([[cg, sg], [-sg, cg]])
     core_cos, core_sin = cos[:, APRON : APRON + TILE], sin[:, APRON : APRON + TILE]
@@ -53,7 +61,7 @@
     lift = lift / GRID
     return [
         np.ascontiguousarray(t).astype(ml_dtypes.bfloat16)
-        for t in (spread, edges, rows, coarse, coarse.T, lift, lift.T, fine, back)
+        for t in (spread, edges, mirror, rows, coarse, coarse.T, lift, lift.T, fine, back)
     ]
 
 
@@ -231,17 +239,18 @@
         grad = dot(back[...], jnp.concatenate([v[:, :TILE], v[:, TILE:]], 0))
         here = mask[t.slot]
         trans = jnp.tanh(0.5 * here)
-        result[t.i] = here - grad * (1.0 - trans * trans)
+        result[t.home] = here - grad * (1.0 - trans * trans)
 
     class Tile:
         def __init__(self, i, lane):
-            self.i, self.lane = i, lane
-            self.slot = slot_ref[i]
+            self.home, self.lane = i, lane
+            self.i = jnp.minimum(i, count - 1)
+            self.slot = slot_ref[self.i]
             self.r = pl.multiple_of(self.slot // COLS * TILE, TILE)
 
     def batch(b, _):
         start = b * LANES
-        tiles = [Tile(jnp.minimum(start + n, count - 1), n) for n in range(LANES)]
+        tiles = [Tile(start + n, n) for n in range(LANES)]
         for t in tiles:
             spectrum(t)
         for t in tiles:
@@ -256,9 +265,11 @@
             resist(t)
         for t in tiles:
             adjoint(t, 0)
-        for t in tiles:
+        for n, t in enumerate(tiles):
             finish(t)
-        for n in range(LANES):
+            if n == 0:
+                out_copy(start).start()
+                continue
 
             @pl.when(start + n < count)
             def _(n=n):
@@ -317,6 +328,7 @@
 CORNERS = ((-1, -1), (-1, 1), (1, -1), (1, 1))
 SIDES = ((-1, 0), (1, 0), (0, -1), (0, 1)) + CORNERS
 CHUNK = 256
+LATER = 8
 CHUNKS = ROWS_HERE // CHUNK
 HALF = ROWS_HERE // 2
 
@@ -336,23 +348,34 @@
     mask_hbm,
     spread_hbm,
     edges_hbm,
-    out,
-    mask,
-    spread,
-    edges,
-    rows_out,
-    cols_out,
-    corners_out,
-    rows_got,
-    cols_got,
-    corners_got,
-    part,
-    strip_sem,
-    table_sem,
-    chunk_sem,
-    send_sem,
-    recv_sem,
+    mirror_hbm,
+    *rest,
 ):
+    later_in, out, later_out, rest = (
+        rest[:LATER],
+        rest[LATER],
+        rest[LATER + 1 : 2 * LATER + 1],
+        rest[2 * LATER + 1 :],
+    )
+    (
+        mask,
+        spread,
+        edges,
+        mirror,
+        rows_out,
+        cols_out,
+        corners_out,
+        rows_got,
+        cols_got,
+        corners_got,
+        part,
+        strip_sem,
+        table_sem,
+        chunk_sem,
+        later_sem,
+        send_sem,
+        recv_sem,
+    ) = rest
     row, col = lax.axis_index("trow"), lax.axis_index("tcol")
 
     def near(dr, dc):
@@ -382,7 +405,12 @@
         chunks.append(load(top, height, SIDE, COLS_HERE - 2 * SIDE, chunk_sem.at[n]))
     near_table = pltpu.make_async_copy(spread_hbm, spread, table_sem.at[0])
     edge_table = pltpu.make_async_copy(edges_hbm, edges, table_sem.at[1])
-    for copy in strips[:2] + [near_table] + strips[2:] + chunks[:1] + [edge_table] + chunks[1:]:
+    mirror_table = pltpu.make_async_copy(mirror_hbm, mirror, table_sem.at[2])
+    laters = [
+        pltpu.make_async_copy(later_in[n], later_out[n], later_sem.at[n]) for n in range(LATER)
+    ]
+    loads = strips[:2] + [near_table] + strips[2:] + chunks[:1] + [edge_table, mirror_table] + chunks[1:]
+    for copy in loads:
         copy.start()
 
     inside_r = [(row > 0).astype(F32), (row < n_rows - 1).astype(F32)]
@@ -408,9 +436,16 @@
             cut = band[:, begin : begin + SIDE] * inside_c[other]
             corners_out[2 * side + other] = packed(cut, other)
     near_table.wait()
+    lanes = lax.broadcasted_iota(jnp.int32, (2 * APRON, FREQ), 1)
+    zero = jnp.zeros((2 * APRON, FREQ), F32)
     for c, piece in enumerate(near_transform(jnp.concatenate(bands, 0), spread)):
+        even, odd = piece[:, :FREQ], piece[:, FREQ:]
+        low = jnp.where(lanes < FREQ // 2, even, pltpu.roll(odd, FREQ // 2, 1)).astype(BF)
+        zero = jnp.where(lanes == c, pltpu.roll(even, FREQ // 2 + c, 1), zero)
         for side in range(2):
-            rows_out[side, c] = piece[side * APRON : (side + 1) * APRON].astype(BF)
+            rows_out[side, c] = low[side * APRON : (side + 1) * APRON]
+    for side in range(2):
+        rows_out[side, COLS] = zero[side * APRON : (side + 1) * APRON].astype(BF)
 
     sources = [rows_out.at[0], rows_out.at[1], cols_out.at[0], cols_out.at[1]]
     places = [rows_got.at[1], rows_got.at[0], cols_got.at[1], cols_got.at[0]]
@@ -440,6 +475,8 @@
         cols_out[side] = packed(band, side)
     for send in sends[2:4]:
         send.start()
+    for copy in laters:
+        copy.start()
 
     for n in range(CHUNKS):
         chunks[n].wait()
@@ -462,35 +499,47 @@
     sends[1].wait()
     for send in sends[4:]:
         send.wait()
+    mirror_table.wait()
+    packs = []
+    for side in range(2):
+        zero = rows_got[side, COLS].astype(F32)
+        for c in range(COLS):
+            lane = jnp.where(lanes[:APRON] == c, zero, 0.0).astype(BF)
+            packs.append(jnp.concatenate([rows_got[side, c], lane], 1))
+    whole = dot(jnp.concatenate(packs, 0), mirror[...])
     for side in range(2):
         start = side * (APRON + ROWS_HERE)
         for c in range(COLS):
-            value = rows_got[side, c]
+            first = (side * COLS + c) * APRON
+            value = whole[first : first + APRON]
             other = {0: 0, COLS - 1: 1}.get(c)
             if other is not None:
                 got = corners_got[2 * side + other]
                 corner = [dot(got, edges[other, h]) for h in range(2)]
-                corner = jnp.concatenate(corner, 0)
-                value = (value.astype(F32) + corner).astype(BF)
-            out[c, start : start + APRON] = value
-
-
-def half_transform(mask, spread, edges, n_rows, n_cols):
+                value = value + jnp.concatenate(corner, 0)
+            out[c, start : start + APRON] = value.astype(BF)
+    for copy in laters:
+        copy.wait()
+
+
+def half_transform(mask, spread, edges, mirror, later, n_rows, n_cols):
     vmem = pl.BlockSpec(memory_space=pltpu.VMEM)
     dma = pltpu.SemaphoreType.DMA
     here = pltpu.with_memory_space_constraint
-    rows_shape = (2, COLS, APRON, 2 * FREQ)
+    rows_shape = (2, COLS + 1, APRON, FREQ)
     cols_shape = (2, HALF, SIDE)
     corners_shape = (len(CORNERS), APRON // 2, SIDE)
     return pl.pallas_call(
         functools.partial(margin_kernel, n_rows, n_cols),
-        out_shape=pltpu.VMEM((COLS, ROWS_HERE + 2 * APRON, 2 * FREQ), BF),
-        in_specs=[pl.BlockSpec(memory_space=pltpu.HBM)] * 3,
-        out_specs=vmem,
+        out_shape=[pltpu.VMEM((COLS, ROWS_HERE + 2 * APRON, 2 * FREQ), BF)]
+        + [pltpu.VMEM(a.shape, a.dtype) for a in later],
+        in_specs=[pl.BlockSpec(memory_space=pltpu.HBM)] * (4 + LATER),
+        out_specs=[vmem] * (1 + LATER),
         scratch_shapes=[
             pltpu.VMEM((ROWS_HERE, COLS_HERE), F32),
             pltpu.VMEM((WIDE, 2 * FREQ), BF),
             pltpu.VMEM((2, 2, SIDE, 2 * FREQ), BF),
+            pltpu.VMEM((2 * FREQ, 2 * FREQ), BF),
             pltpu.VMEM(rows_shape, BF),
             pltpu.VMEM(cols_shape, BF),
             pltpu.VMEM(corners_shape, BF),
@@ -499,8 +548,9 @@
             pltpu.VMEM(corners_shape, BF),
             pltpu.VMEM((2, ROWS_HERE, 2 * FREQ), F32),
             dma((4,)),
-            dma((2,)),
+            dma((3,)),
             dma((CHUNKS,)),
+            dma((LATER,)),
             dma((len(SIDES),)),
             dma((len(SIDES),)),
         ],
@@ -510,13 +560,19 @@
         cost_estimate=pl.CostEstimate(
             flops=2_000_000_000, bytes_accessed=10_000_000, transcendentals=2_000_000
         ),
-    )(*[here(a, pltpu.HBM) for a in (mask, spread, edges)])
+    )(*[here(a, pltpu.HBM) for a in (mask, spread, edges, mirror, *later)])
 
 
 def body(mask_level, target, kernels, step_sizes, density_class, work_list):
-    spread, edges, *tabs = [jnp.asarray(t) for t in tables()]
-    half_spectra = half_transform(
-        mask_level, spread, edges, lax.axis_size("trow"), lax.axis_size("tcol")
+    spread, edges, mirror, *tabs = [jnp.asarray(t) for t in tables()]
+    half_spectra, kernels, *tabs = half_transform(
+        mask_level,
+        spread,
+        edges,
+        mirror,
+        [kernels, *tabs],
+        lax.axis_size("trow"),
+        lax.axis_size("tcol"),
     )
     return take_step(density_class, step_sizes, mask_level, target, half_spectra, kernels, tabs)
 

time: 33.1 us -> 30.8 us (0.931)
  the two profiles are of different devices: /device:TPU:6 before, /device:TPU:4 now
where the time goes in v6:
time: 30.8 us; the launch traced here: 30.7 us
  Pallas kernels  30.7 us (100%)
    pallas_call x1, Pallas kernels, take_step(): pl.pallas_call(step_kernel, out_shape=jax.ShapeDtypeStruct((ROWS_HERE, CO...  18.2 us
    pallas_call x1, Pallas kernels, half_transform(): pl.pallas_call(functools.partial(margin_kernel, n_rows, n_cols), out_shap...  12.5 us

profile of v6, /device:TPU:4, one launch (start us, length us, event | category | flops | bytes accessed | tf_op | source)
XLA Modules:
  0.0 30.7 jit_solution(4817138019096825350)
XLA Ops:
  0.0 0.0 copy-start
  0.0 0.0 copy-start.1
  0.0 12.5 %shard_map.145 = (bf16[4,1152,256]{2,1,0:T(8,128)(2,1)S(1)}, f32[12,2,128,128]{3,2,1,0:T(8,128)S(1)}, bf16[256,640]{1,0:T(8,128)(2,1)S(1)}, bf16[256,512]{1,0:T(...) custom-call(f32[1024,2048]{1,0:T(8,128)} %mask_hbm.3, ...), custom_call_target="tpu_custom_call" | custom-call | flops 2000000000 | bytes 10000000 | tf_op jit(solution)/shard_map/pallas_call | solution.py:532
  12.5 0.0 copy-done
  12.5 0.0 copy-done.1
  12.5 18.2 %shard_map.146 = f32[1024,2048]{1,0:T(8,128)} custom-call(s32[2,4]{1,0:T(2,128)S(1)} %copy-done, f32[3]{0:T(128)S(1)} %copy-done.1, f32[1024,2048]{1,0:T(8,128)} %mask_hbm.3, bf16[1024,2048]{1,0:T(8,128)(2,1)} %target_hbm.1, bf16[4,1152,256]{2,1,0:T(8,128)(2,1)S(1)} %get-tuple-element.14.half_spectra, f32[12,2,128,128]{3,2,1,0:T(8,128)S(1)} %get-tuple-element.15.kern, ...), custom_call_target="tpu_custom_call" | custom-call | flops 30000001024 | bytes 40000000 | tf_op jit(solution)/shard_map/pallas_call | solution.py:296
Async XLA Ops:
  0.0 12.5 %copy-start = (s32[2,4]{1,0:T(2,128)S(1)}, s32[2,4]{1,0:T(2,128)}, u32[]{:S(2)}) copy-start(s32[2,4]{1,0:T(2,128)} %cls_ref.1) | copy-start | bytes 100
  0.0 12.5 %copy-start.1 = (f32[3]{0:T(128)S(1)}, f32[3]{0:T(128)}, u32[]{:S(2)}) copy-start(f32[3]{0:T(128)} %steps_ref.1) | copy-start | bytes 40

commit v7 on v6

--- a/solution.py
+++ b/solution.py
@@ -327,7 +327,7 @@
 
 CORNERS = ((-1, -1), (-1, 1), (1, -1), (1, 1))
 SIDES = ((-1, 0), (1, 0), (0, -1), (0, 1)) + CORNERS
-CHUNK = 256
+CHUNK = 512
 LATER = 8
 CHUNKS = ROWS_HERE // CHUNK
 HALF = ROWS_HERE // 2

time: 30.8 us -> 30.7 us (level)
  the two profiles are of different devices: /device:TPU:4 before, /device:TPU:2 now
where the time goes in v7:
time: 30.7 us; the launch traced here: 30.6 us
  Pallas kernels  30.5 us (99%)
    pallas_call x1, Pallas kernels, take_step(): pl.pallas_call(step_kernel, out_shape=jax.ShapeDtypeStruct((ROWS_HERE, CO...  18.7 us
    pallas_call x1, Pallas kernels, half_transform(): pl.pallas_call(functools.partial(margin_kernel, n_rows, n_cols), out_shap...  11.8 us

profile of v7, /device:TPU:2, one launch (start us, length us, event | category | flops | bytes accessed | tf_op | source)
XLA Modules:
  0.0 30.6 jit_solution(7837185942154500003)
XLA Ops:
  0.0 0.0 copy-start
  0.0 0.0 copy-start.1
  0.0 11.8 %shard_map.145 = (bf16[4,1152,256]{2,1,0:T(8,128)(2,1)S(1)}, f32[12,2,128,128]{3,2,1,0:T(8,128)S(1)}, bf16[256,640]{1,0:T(8,128)(2,1)S(1)}, bf16[256,512]{1,0:T(...) custom-call(f32[1024,2048]{1,0:T(8,128)} %mask_hbm.3, ...), custom_call_target="tpu_custom_call" | custom-call | flops 2000000000 | bytes 10000000 | tf_op jit(solution)/shard_map/pallas_call | solution.py:532
  11.8 0.0 copy-done
  11.8 0.0 copy-done.1
  11.9 18.7 %shard_map.146 = f32[1024,2048]{1,0:T(8,128)} custom-call(s32[2,4]{1,0:T(2,128)S(1)} %copy-done, f32[3]{0:T(128)S(1)} %copy-done.1, f32[1024,2048]{1,0:T(8,128)} %mask_hbm.3, bf16[1024,2048]{1,0:T(8,128)(2,1)} %target_hbm.1, bf16[4,1152,256]{2,1,0:T(8,128)(2,1)S(1)} %get-tuple-element.14.half_spectra, f32[12,2,128,128]{3,2,1,0:T(8,128)S(1)} %get-tuple-element.15.kern, ...), custom_call_target="tpu_custom_call" | custom-call | flops 30000001024 | bytes 40000000 | tf_op jit(solution)/shard_map/pallas_call | solution.py:296
Async XLA Ops:
  0.0 11.8 %copy-start = (s32[2,4]{1,0:T(2,128)S(1)}, s32[2,4]{1,0:T(2,128)}, u32[]{:S(2)}) copy-start(s32[2,4]{1,0:T(2,128)} %cls_ref.1) | copy-start | bytes 100
  0.0 11.8 %copy-start.1 = (f32[3]{0:T(128)S(1)}, f32[3]{0:T(128)}, u32[]{:S(2)}) copy-start(f32[3]{0:T(128)} %steps_ref.1) | copy-start | bytes 40
